TPU v7x, 32 devices: a whole 2x2x4 slice. The times are simulated.
32 devices in a mesh: sub: 16 (over z, y, core), row: 2 (over x).
Axes of the slice: x: 2, y: 2, z: 4, core: 2. Of those that a mesh axis runs over, the one named last changes fastest.
Arguments:
- compliance: bfloat16 [16, 36, 18, 128, 128], P('sub', 'row'), may hold values from -0.0625 to 0.0625
- block_columns: int32 [16, 36, 18], P('sub', 'row'), may hold values from 0 to 35, as said below
- load_response: bfloat16 [16, 32, 4608], P('sub', None, 'row'), may hold values from -6 to 6
- starting_motion: bfloat16 [16, 32, 4608], P('sub', None, 'row'), may hold values from -6 to 6
- start_traction: bfloat16 [16, 32, 4608], P('sub', None, 'row'), may hold values from -6 to 6
- stiffness: float32 [16, 4608], P('sub', 'row'), may hold values from 1 to 10
- history: float32 [16, 4608], P('sub', 'row'), may hold values from 0 to 0.6
- face_partner: int32 [16, 36], P('sub', 'row'), may hold values from -1 to 8, as said below
- orientation: int32 [16, 36, 128], P('sub', 'row'), may hold values from 0 to 127, as said below
Outputs:
- displacement: bfloat16 [16, 32, 4608], P('sub', None, 'row')
- traction: bfloat16 [16, 32, 4608], P('sub', None, 'row')
Inputs may be any that keep to these rules, and one draw needn't show every extreme that they name: `block_columns`: each block row names 18 distinct face columns. `face_partner`: an entry is -1 for a free face, else the position, within the facing group of the same run of the neighbouring substructure, of the matched face. Matches are mutual. Faces facing s+1 on the last substructure and faces facing s-1 on the first are free. In some run of some substructure all 9 faces facing s+1 are matched. `orientation`: each face's row is a permutation of 0 to 127; matched faces carry mutually inverse permutations.
All inputs are finite; a program needn't handle non-finite values.
Results may differ from a plain program's by a relative error of at most 0.0045.
The roundings to bfloat16 on the way count: a program that leaves them out, or rounds other values in their place, can miss the bound.
Values may be sent and summed in bfloat16 or wider, within the bound.
No kernel may reach another device: no remote copies, remote signals or barrier semaphores. Data moves between devices by JAX's collectives and lax.ppermute only.
A program may use at most 64 MiB of HBM per device.

v0:
```python
import jax
import jax.numpy as jnp
from jax import lax
from jax.sharding import PartitionSpec as P

SURFACE_EXTENT = 128
ITERS = 3


search_stiffness = 1.0
onset_jump = 0.15
failure_jump = 1.5


def passed_along(value, axis, steps):
    count = lax.axis_size(axis)
    first, last = (max(0, -steps), min(count, count - steps))
    return lax.ppermute(value, axis, [(source, source + steps) for source in range(first, last)])


def cohesive(upward_marker, constitutive_parameters, opposing_surface, live_mask):
    temporal_points = upward_marker.shape[0]
    mate_upward_marker = opposing_surface[:temporal_points]
    joint_rigidity = 0.5 * (constitutive_parameters[0] + opposing_surface[temporal_points])
    joint_record = jnp.maximum(constitutive_parameters[1], opposing_surface[temporal_points + 1])
    difference = upward_marker - mate_upward_marker
    jump_size = difference / (search_stiffness + 2.0 * joint_rigidity)
    running_peak = lax.associative_scan(jnp.maximum, jnp.abs(jump_size), axis=0)
    peak_jump = jnp.maximum(joint_record, running_peak)
    damage = jnp.clip((peak_jump - onset_jump) / (failure_jump - onset_jump), 0.0, 1.0)
    effective = joint_rigidity * (1.0 - damage)
    traction = jnp.where(
        live_mask, effective * difference / (search_stiffness + 2.0 * effective), 0.0
    )
    displacement = (traction - upward_marker) / search_stiffness
    return (displacement, traction)


def shards(
    compliance,
    block_columns,
    load_response,
    starting_motion,
    start_traction,
    stiffness,
    history,
    face_partner,
    orientation,
):
    compliance_rows = compliance[0]
    columns = block_columns[0]
    temporal_points = starting_motion.shape[1]
    segment_breadth = starting_motion.shape[2]
    number_surfaces = segment_breadth // SURFACE_EXTENT
    group_size = number_surfaces // 2
    stored_blocks = columns.shape[1]
    applied_forces = load_response[0].astype(jnp.float32)
    constitutive_parameters = jnp.stack([stiffness[0], history[0]]).reshape(
        2, number_surfaces, SURFACE_EXTENT
    )
    partner_table = face_partner[0]
    turning = orientation[0]
    turn_table = (
        turning[:, :, None] == jnp.arange(SURFACE_EXTENT, dtype=jnp.int32)[None, None, :]
    ).astype(jnp.float32)
    facing_up = jnp.arange(number_surfaces) < group_size
    live_mask = (partner_table >= 0)[:, None]
    safe_index = jnp.maximum(partner_table, 0)
    source = jnp.where(facing_up, safe_index, group_size + safe_index)
    present_motion = starting_motion[0].astype(jnp.float32)
    present_stress = start_traction[0].astype(jnp.float32)
    for iteration in range(ITERS):
        robin_sum = present_stress + search_stiffness * present_motion
        gathered_entries = lax.all_gather(robin_sum.astype(jnp.bfloat16), "row", axis=1, tiled=True)
        flexibility_tiles = gathered_entries.reshape(temporal_points, -1, SURFACE_EXTENT)

        def add_block(index, total):
            column_slice = lax.dynamic_index_in_dim(columns, index, 1, keepdims=False)
            piece = jnp.take(flexibility_tiles, column_slice, axis=1)
            block = lax.dynamic_index_in_dim(compliance_rows, index, 1, keepdims=False)
            return total + jnp.einsum(
                "tib,iab->tia", piece, block, preferred_element_type=jnp.float32
            )

        starting_total = jnp.zeros((temporal_points, number_surfaces, SURFACE_EXTENT), jnp.float32)
        operator_multiply = lax.fori_loop(0, stored_blocks, add_block, starting_total)
        proportional_reaction = (
            operator_multiply.reshape(temporal_points, segment_breadth) + applied_forces
        )
        upward_marker = (robin_sum - 2.0 * search_stiffness * proportional_reaction).reshape(
            temporal_points, number_surfaces, SURFACE_EXTENT
        )
        payload = jnp.concatenate([upward_marker, constitutive_parameters], axis=0)[None]
        below_faces = passed_along(payload[:, :, :group_size], "sub", 1)[0]
        above_faces = passed_along(payload[:, :, group_size:], "sub", -1)[0]
        combined = jnp.concatenate([above_faces, below_faces], axis=1)
        chosen = jnp.take(combined, source, axis=1)
        opposing_surface = jnp.einsum(
            "tfy,fxy->tfx", chosen, turn_table, precision=lax.Precision.HIGHEST
        )
        motion_distribution, stress_distribution = cohesive(
            upward_marker, constitutive_parameters, opposing_surface, live_mask
        )
        present_motion = motion_distribution.reshape(temporal_points, segment_breadth)
        present_stress = stress_distribution.reshape(temporal_points, segment_breadth)
    return (present_motion.astype(jnp.bfloat16)[None], present_stress.astype(jnp.bfloat16)[None])


def solution(mesh):
    in_specs = (
        P("sub", "row", None, None, None),
        P("sub", "row", None),
        P("sub", None, "row"),
        P("sub", None, "row"),
        P("sub", None, "row"),
        P("sub", "row"),
        P("sub", "row"),
        P("sub", "row"),
        P("sub", "row", None),
    )
    out_specs = (P("sub", None, "row"), P("sub", None, "row"))
    return jax.shard_map(shards, mesh=mesh, in_specs=in_specs, out_specs=out_specs, check_vma=False)
```

profile of v0, /device:TPU:13, one launch (start us, length us, event | category | flops | bytes accessed | tf_op | source)
XLA Modules:
  0.0 196.0 jit_solution(3431752376327346118)
XLA Ops:
  1.7 9.7 %copy.62 = bf16[1,18,18,128,128]{4,3,1,2,0:T(8,128)(2,1)} copy(bf16[1,18,18,128,128]{4,3,2,1,0:T(8,128)(2,1)} %param.19) | data formatting | bytes 21233664 | tf_op args[0]
  11.5 5.4 %all-gather = bf16[1,32,4608]{2,1,0:T(8,128)(2,1)S(1)} all-gather(bf16[1,32,2304]{2,1,0:T(8,128)(2,1)S(1)} %get-tuple-element.417), channel_id=2, replica_groups=mesh['sub'=16,'row'=2] {'row'}, dimensions={2}, use_global_device_ids=true | all-gather | bytes 442368 | tf_op jit(solution)/shard_map/all_gather | solution.py:74
  17.1 38.6 %while.42 = (s32[]{:T(128)}, f32[32,18,128]{2,0,1:T(8,128)S(1)}, bf16[18,18,128,128]{3,2,0,1:T(8,128)(2,1)}, s32[18,18]{0,1:T(8,128)S(1)}, bf16[32,36,128]{2,0,1:T(8,128)(2,1)S(1)}, /*index=5*/s32[]{:T(128)}, s32[]{:T(128)}) while((s32[]{:T(128)}, f32[32,18,128]{2,0,1:T(8,128)S(1)}, bf16[18,18,128,128]{3,2,0,1:T(8,128)(2,1)}, ...), condition=%wide.region_1.0_spmd.clone, body=%wide.region_0.2_spmd.clone.sunk | while | flops 19096688 | bytes 1626539 | solution.py:86
  17.8 1.5 fusion.75
  19.9 1.5 fusion.75
  22.1 1.5 fusion.75
  24.2 1.5 fusion.75
  26.4 1.5 fusion.75
  28.5 1.5 fusion.75
  30.7 1.5 fusion.75
  32.8 1.5 fusion.75
  35.0 1.5 fusion.75
  37.1 1.5 fusion.75
  43.5 1.5 fusion.75
  56.2 4.6 %collective-permute-start.1 = (f32[1,34,9,128]{3,1,2,0:T(8,128)S(1)}, f32[1,34,9,128]{3,1,2,0:T(8,128)S(1)}, u32[]{:S(2)}, u32[]{:S(2)}) collective-permute-start(f32[1,34,9,128]{3,1,2,0:T(8,128)S(1)} %get-tuple-element.416), channel_id=1, source_target_pairs={{0,2},{2,4},{4,6},{6,8},{8,10},{10,12},{12,14},{14,16},{16,18},{18... | collective-permute-start | bytes 470024 | tf_op jit(solution)/shard_map/ppermute | solution.py:18
  60.7 1.9 collective-permute-start
  63.2 5.3 %collective-permute-done = f32[1,34,9,128]{3,1,2,0:T(8,128)S(1)} collective-permute-done((f32[1,34,9,128]{3,1,2,0:T(8,128)S(1)}, f32[1,34,9,128]{3,1,2,0:T(8,128)S(1)}, u32[]{:S(2)}, u32[]{:S(2)}) %collective-permute-start) | collective-permute-done | bytes 156704 | tf_op jit(solution)/shard_map/ppermute | solution.py:18
  69.1 1.7 convolution_bitcast_fusion.5
  73.6 4.7 %all_gather.10 = bf16[32,4608]{1,0:T(8,128)(2,1)S(1)} all-gather(bf16[32,2304]{1,0:T(8,128)(2,1)S(1)} %bitcast.166), channel_id=1, replica_groups=mesh['sub'=16,'row'=2] {'row'}, dimensions={1}, use_global_device_ids=true | all-gather | bytes 442368 | tf_op jit(solution)/shard_map/all_gather | solution.py:74
  78.3 38.6 %while.43 = (s32[]{:T(128)}, f32[32,18,128]{2,0,1:T(8,128)S(1)}, bf16[18,18,128,128]{3,2,0,1:T(8,128)(2,1)}, s32[18,18]{0,1:T(8,128)S(1)}, bf16[32,36,128]{2,0,1:T(8,128)(2,1)S(1)}, /*index=5*/s32[]{:T(128)}, s32[]{:T(128)}) while((s32[]{:T(128)}, f32[32,18,128]{2,0,1:T(8,128)S(1)}, bf16[18,18,128,128]{3,2,0,1:T(8,128)(2,1)}, ...), condition=%wide.region_3.6_spmd.clone, body=%wide.region_2.5_spmd.clone.sunk | while | flops 19096688 | bytes 1626539 | solution.py:86
  109.0 1.5 fusion.78
  117.1 4.4 %collective-permute-start.3 = (f32[1,34,9,128]{3,1,2,0:T(8,128)S(1)}, f32[1,34,9,128]{3,1,2,0:T(8,128)S(1)}, u32[]{:S(2)}, u32[]{:S(2)}) collective-permute-start(f32[1,34,9,128]{3,1,2,0:T(8,128)S(1)} %get-tuple-element.413), channel_id=1, source_target_pairs={{0,2},{2,4},{4,6},{6,8},{8,10},{10,12},{12,14},{14,16},{16,18},{18... | collective-permute-start | bytes 470024 | tf_op jit(solution)/shard_map/ppermute | solution.py:18
  121.5 1.9 collective-permute-start.2
  124.0 5.3 %collective-permute-done.2 = f32[1,34,9,128]{3,1,2,0:T(8,128)S(1)} collective-permute-done((f32[1,34,9,128]{3,1,2,0:T(8,128)S(1)}, f32[1,34,9,128]{3,1,2,0:T(8,128)S(1)}, u32[]{:S(2)}, u32[]{:S(2)}) %collective-permute-start.2) | collective-permute-done | bytes 156704 | tf_op jit(solution)/shard_map/ppermute | solution.py:18
  129.9 1.7 convolution_bitcast_fusion.4
  134.4 4.7 %all_gather.11 = bf16[32,4608]{1,0:T(8,128)(2,1)S(1)} all-gather(bf16[32,2304]{1,0:T(8,128)(2,1)S(1)} %bitcast.167), channel_id=1, replica_groups=mesh['sub'=16,'row'=2] {'row'}, dimensions={1}, use_global_device_ids=true | all-gather | bytes 442368 | tf_op jit(solution)/shard_map/all_gather | solution.py:74
  139.1 38.6 %while.44 = (s32[]{:T(128)}, f32[32,18,128]{2,0,1:T(8,128)S(1)}, bf16[18,18,128,128]{3,2,0,1:T(8,128)(2,1)}, s32[18,18]{0,1:T(8,128)S(1)}, bf16[32,36,128]{2,0,1:T(8,128)(2,1)S(1)}, /*index=5*/s32[]{:T(128)}, s32[]{:T(128)}) while((s32[]{:T(128)}, f32[32,18,128]{2,0,1:T(8,128)S(1)}, bf16[18,18,128,128]{3,2,0,1:T(8,128)(2,1)}, ...), condition=%wide.region_5.8_spmd.clone, body=%wide.region_4.7_spmd.clone.sunk | while | flops 19096688 | bytes 1626539 | solution.py:86
  144.0 1.5 fusion.81
  177.9 3.5 %collective-permute-start.5 = (f32[1,34,9,128]{3,1,2,0:T(8,128)S(1)}, f32[1,34,9,128]{3,1,2,0:T(8,128)S(1)}, u32[]{:S(2)}, u32[]{:S(2)}) collective-permute-start(f32[1,34,9,128]{3,1,2,0:T(8,128)S(1)} %get-tuple-element.410), channel_id=1, source_target_pairs={{0,2},{2,4},{4,6},{6,8},{8,10},{10,12},{12,14},{14,16},{16,18},{18... | collective-permute-start | bytes 470024 | tf_op jit(solution)/shard_map/ppermute | solution.py:18
  181.5 1.9 collective-permute-start.4
  184.0 5.3 %collective-permute-done.4 = f32[1,34,9,128]{3,1,2,0:T(8,128)S(1)} collective-permute-done((f32[1,34,9,128]{3,1,2,0:T(8,128)S(1)}, f32[1,34,9,128]{3,1,2,0:T(8,128)S(1)}, u32[]{:S(2)}, u32[]{:S(2)}) %collective-permute-start.4) | collective-permute-done | bytes 156704 | tf_op jit(solution)/shard_map/ppermute | solution.py:18
  189.9 1.7 convolution_bitcast_fusion.3
  (390 shorter events, 109.0 us)
Async XLA Ops:
  1.7 9.7 %copy-start.3 = (s32[1,18,18]{2,0,1:T(1,128)S(1)}, s32[1,18,18]{2,0,1:T(1,128)}, u32[]{:S(2)}) copy-start(s32[1,18,18]{2,0,1:T(1,128)} %param.20) | copy-start | bytes 3892
  1.7 54.1 %copy-start = (bf16[1,32,2304]{2,1,0:T(8,128)(2,1)S(1)}, bf16[1,32,2304]{2,1,0:T(8,128)(2,1)}, u32[]{:S(2)}) copy-start(bf16[1,32,2304]{2,1,0:T(8,128)(2,1)} %param.21) | copy-start | bytes 442372
  11.4 44.5 %copy-start.1 = (f32[1,2304]{1,0:T(1,128)S(1)}, f32[1,2304]{1,0:T(1,128)}, u32[]{:S(2)}) copy-start(f32[1,2304]{1,0:T(1,128)} %param.25) | copy-start | bytes 27652
  11.4 44.5 %copy-start.2 = (f32[1,2304]{1,0:T(1,128)S(1)}, f32[1,2304]{1,0:T(1,128)}, u32[]{:S(2)}) copy-start(f32[1,2304]{1,0:T(1,128)} %param.24) | copy-start | bytes 27652
  11.4 51.2 %copy-start.5 = (s32[1,18]{1,0:T(1,128)S(1)}, s32[1,18]{1,0:T(1,128)}, u32[]{:S(2)}) copy-start(s32[1,18]{1,0:T(1,128)} %param.26) | copy-start | bytes 220
  11.4 51.3 %copy-start.4 = (s32[1,18,128]{2,0,1:T(1,128)S(1)}, s32[1,18,128]{2,0,1:T(1,128)}, u32[]{:S(2)}) copy-start(s32[1,18,128]{2,0,1:T(1,128)} %param.27) | copy-start | bytes 27652
  56.2 7.0 %collective-permute-start.1 = (f32[1,34,9,128]{3,1,2,0:T(8,128)S(1)}, f32[1,34,9,128]{3,1,2,0:T(8,128)S(1)}, u32[]{:S(2)}, u32[]{:S(2)}) collective-permute-start(f32[1,34,9,128]{3,1,2,0:T(8,128)S(1)} %get-tuple-element.416), channel_id=1, source_target_pairs={{0,2},{2,4},{4,6},{6,8},{8,10},{10,12},{12,14},{14,16},{16,18},{18... | collective-permute-start | bytes 470024 | tf_op jit(solution)/shard_map/ppermute | solution.py:18
  60.7 7.8 %collective-permute-start = (f32[1,34,9,128]{3,1,2,0:T(8,128)S(1)}, f32[1,34,9,128]{3,1,2,0:T(8,128)S(1)}, u32[]{:S(2)}, u32[]{:S(2)}) collective-permute-start(f32[1,34,9,128]{3,1,2,0:T(8,128)S(1)} %get-tuple-element.415), channel_id=1, source_target_pairs={{2,0},{4,2},{6,4},{8,6},{10,8},{12,10},{14,12},{16,14},{18,16},{20... | collective-permute-start | bytes 470024 | tf_op jit(solution)/shard_map/ppermute | solution.py:18
  117.1 6.9 %collective-permute-start.3 = (f32[1,34,9,128]{3,1,2,0:T(8,128)S(1)}, f32[1,34,9,128]{3,1,2,0:T(8,128)S(1)}, u32[]{:S(2)}, u32[]{:S(2)}) collective-permute-start(f32[1,34,9,128]{3,1,2,0:T(8,128)S(1)} %get-tuple-element.413), channel_id=1, source_target_pairs={{0,2},{2,4},{4,6},{6,8},{8,10},{10,12},{12,14},{14,16},{16,18},{18... | collective-permute-start | bytes 470024 | tf_op jit(solution)/shard_map/ppermute | solution.py:18
  121.5 7.8 %collective-permute-start.2 = (f32[1,34,9,128]{3,1,2,0:T(8,128)S(1)}, f32[1,34,9,128]{3,1,2,0:T(8,128)S(1)}, u32[]{:S(2)}, u32[]{:S(2)}) collective-permute-start(f32[1,34,9,128]{3,1,2,0:T(8,128)S(1)} %get-tuple-element.412), channel_id=1, source_target_pairs={{2,0},{4,2},{6,4},{8,6},{10,8},{12,10},{14,12},{16,14},{18,16},{20... | collective-permute-start | bytes 470024 | tf_op jit(solution)/shard_map/ppermute | solution.py:18
  177.9 6.0 %collective-permute-start.5 = (f32[1,34,9,128]{3,1,2,0:T(8,128)S(1)}, f32[1,34,9,128]{3,1,2,0:T(8,128)S(1)}, u32[]{:S(2)}, u32[]{:S(2)}) collective-permute-start(f32[1,34,9,128]{3,1,2,0:T(8,128)S(1)} %get-tuple-element.410), channel_id=1, source_target_pairs={{0,2},{2,4},{4,6},{6,8},{8,10},{10,12},{12,14},{14,16},{16,18},{18... | collective-permute-start | bytes 470024 | tf_op jit(solution)/shard_map/ppermute | solution.py:18
  181.5 7.8 %collective-permute-start.4 = (f32[1,34,9,128]{3,1,2,0:T(8,128)S(1)}, f32[1,34,9,128]{3,1,2,0:T(8,128)S(1)}, u32[]{:S(2)}, u32[]{:S(2)}) collective-permute-start(f32[1,34,9,128]{3,1,2,0:T(8,128)S(1)} %get-tuple-element.409), channel_id=1, source_target_pairs={{2,0},{4,2},{6,4},{8,6},{10,8},{12,10},{14,12},{16,14},{18,16},{20... | collective-permute-start | bytes 470024 | tf_op jit(solution)/shard_map/ppermute | solution.py:18
where the time goes:
time: 199 us; the launch traced here: 196 us
  matrix products  87.2 us (44%)
  local copies, waits for them, and re-layouts  50.4 us (25%)
  starting transfers between devices  18.3 us (9%)
  waiting for transfers between devices  17.4 us (9%)
  blocking collectives  14.7 us (7%)
  other arithmetic  4.5 us (2%)
    dot_general x54, matrix products, add_block(): jnp.einsum('tib,iab->tia', piece, block, preferred_element_type=jnp.float32)  82 us
    gather x54, local copies, waits for them, and re-layouts, add_block(): piece = jnp.take(flexibility_tiles, column_slice, axis=1)  31 us
    ppermute x6, starting transfers between devices, passed_along(): lax.ppermute(value, axis, [(source, source + steps) for source in range(f...  18.3 us
    ppermute x6, waiting for transfers between devices, passed_along(): lax.ppermute(value, axis, [(source, source + steps) for source in range(f...  17.4 us
    all_gather x3, blocking collectives, shards(): lax.all_gather(robin_sum.astype(jnp.bfloat16), 'row', axis=1, tiled=True)  14.7 us
    unnamed x26, local copies, waits for them, and re-layouts  9.97 us
    dot_general x3, matrix products, shards(): jnp.einsum('tfy,fxy->tfx', chosen, turn_table, precision=lax.Precision.HI...  5.16 us
    pad x24, local copies, waits for them, and re-layouts, cohesive(): running_peak = lax.associative_scan(jnp.maximum, jnp.abs(jump_size), axis=0)  3.99 us
  transfers between devices with their start and end apart: 6, of which 6 were waited for; matrix products, arithmetic and copies ran while one was open for 0% of the time, Pallas kernels for 0%

commit v1 on v0

v1 whole, which is shorter than its diff:
```python
import functools

import jax
import jax.numpy as jnp
from jax import lax
from jax.experimental import pallas as pl
from jax.experimental.pallas import tpu as pltpu
from jax.sharding import PartitionSpec as P

ITERS = 3
SUBLANES = 8
VMEM_BYTES = 24 * 2**20

ONSET_JUMP = 0.15
FAILURE_JUMP = 1.5

VMEM = pl.BlockSpec(memory_space=pltpu.VMEM)
SMEM = pl.BlockSpec(memory_space=pltpu.SMEM)


def first_robin(motion_ref, stress_ref, load_ref, turn_ref, stiff_ref, record_ref,
                robin_ref, half_ref, load_faces_ref, turn_out_ref, stiff_out_ref, record_out_ref):
    faces, _, extent = robin_ref.shape
    for face in range(faces):
        lanes = slice(face * extent, (face + 1) * extent)
        robin = stress_ref[:, lanes].astype(jnp.float32) + motion_ref[:, lanes].astype(jnp.float32)
        robin_ref[face] = robin
        half_ref[face] = robin.astype(jnp.bfloat16)
        load_faces_ref[face] = load_ref[:, lanes]
    turn_out_ref[...] = turn_ref[...]
    stiff_out_ref[...] = stiff_ref[...]
    record_out_ref[...] = record_ref[...]


def linear_section(side, columns_ref, place_ref, compliance_ref, own_ref, other_ref, robin_ref, load_ref,
                   stiff_ref, record_ref, out_ref, half_ref):
    group, rows, _ = out_ref.shape
    faces, times, _ = own_ref.shape
    stored = compliance_ref.shape[1]
    first, mine = place_ref[side], place_ref[2]
    half_ref[pl.ds(mine * faces, faces)] = own_ref[...]
    half_ref[pl.ds((1 - mine) * faces, faces)] = other_ref[...]
    for index in range(group):
        face = first + index
        picked = jnp.concatenate([half_ref[columns_ref[face, j]] for j in range(stored)], axis=1)
        blocks = jnp.concatenate([compliance_ref[face, j] for j in range(stored)], axis=1)
        response = lax.dot_general(
            picked, blocks, (((1,), (1,)), ((), ())), preferred_element_type=jnp.float32
        ) + load_ref[face].astype(jnp.float32)
        out_ref[index, :times] = robin_ref[face] - 2.0 * response
        if rows > times:
            out_ref[index, times : times + 1] = stiff_ref[pl.ds(face, 1), :]
            out_ref[index, times + 1 : times + 2] = record_ref[pl.ds(face, 1), :]
            out_ref[index, times + 2 :] = jnp.zeros_like(out_ref[index, times + 2 :])


def running_peak(sizes):
    row = lax.broadcasted_iota(jnp.int32, sizes.shape, 0)
    step = 1
    while step < sizes.shape[0]:
        earlier = pltpu.roll(sizes, step, 0)
        sizes = jnp.maximum(sizes, jnp.where(row >= step, earlier, 0.0))
        step *= 2
    return sizes


def local_section(begin, last, place_ref, partner_ref, turn_ref, own0_ref, own1_ref, mate0_ref, mate1_ref,
                  stiff_ref, record_ref, first_ref, second_ref, *pair_refs):
    group = own0_ref.shape[0]
    times, extent = first_ref.shape[0] if last else first_ref.shape[1], turn_ref.shape[1]
    gather = functools.partial(jnp.take_along_axis, axis=1, mode="promise_in_bounds")
    for side, (own_ref, mate_ref) in enumerate(((own0_ref, mate0_ref), (own1_ref, mate1_ref))):
        for index in range(group):
            face = place_ref[side] + index
            partner = partner_ref[face]
            mate = jnp.maximum(partner, 0)
            turn = turn_ref[pl.ds(face, 1), :]
            ascent = own_ref[index, :times]
            mate_ascent = gather(mate_ref[mate, :times], jnp.broadcast_to(turn, (times, extent)))
            stiffness = stiff_ref[pl.ds(face, 1), :]
            record = record_ref[pl.ds(face, 1), :]
            if begin:
                constants = gather(mate_ref[mate, times:], jnp.broadcast_to(turn, (SUBLANES, extent)))
                stiffness = 0.5 * (stiffness + constants[:1])
                record = jnp.maximum(record, constants[1:2])
                pair_refs[0][pl.ds(face, 1), :] = stiffness
                pair_refs[1][pl.ds(face, 1), :] = record
            difference = ascent - mate_ascent
            jump = difference / (1.0 + 2.0 * stiffness)
            peak = jnp.maximum(record, running_peak(jnp.abs(jump)))
            damage = jnp.clip((peak - ONSET_JUMP) / (FAILURE_JUMP - ONSET_JUMP), 0.0, 1.0)
            effective = stiffness * (1.0 - damage)
            traction = jnp.where(partner >= 0, effective * difference / (1.0 + 2.0 * effective), 0.0)
            motion = traction - ascent
            if last:
                lanes = pl.ds(pl.multiple_of(face * extent, extent), extent)
                first_ref[:, lanes] = motion.astype(jnp.bfloat16)
                second_ref[:, lanes] = traction.astype(jnp.bfloat16)
            else:
                robin = traction + motion
                first_ref[face] = robin
                second_ref[face] = robin.astype(jnp.bfloat16)


def shards(
    compliance,
    block_columns,
    load_response,
    starting_motion,
    start_traction,
    stiffness,
    history,
    face_partner,
    orientation,
):
    _, faces, stored, extent, _ = compliance.shape
    times = starting_motion.shape[1]
    group = faces // 2
    subs = lax.axis_size("sub")
    rows = lax.axis_size("row")
    near = group * (lax.axis_index("sub") % 2)
    place = jnp.stack([near, group - near, lax.axis_index("row")]).astype(jnp.int32)
    near_pairs = [(s, s ^ 1) for s in range(subs) if s ^ 1 < subs]
    far_pairs = [(s, t) for s in range(subs) for t in [s - 1 if s % 2 == 0 else s + 1] if 0 <= t < subs]
    swap = [(r, rows - 1 - r) for r in range(rows)]
    params = pltpu.CompilerParams(vmem_limit_bytes=VMEM_BYTES)

    compliance = pltpu.with_memory_space_constraint(compliance[0], pltpu.VMEM)
    columns = block_columns[0]
    partner = face_partner[0]

    def f32(*shape):
        return jax.ShapeDtypeStruct(shape, jnp.float32)

    def bf16(*shape):
        return jax.ShapeDtypeStruct(shape, jnp.bfloat16)

    tall = (faces, times, extent)
    robin, half, load, turn, stiff, record = pl.pallas_call(
        first_robin,
        out_shape=(
            f32(*tall), bf16(*tall), bf16(*tall),
            jax.ShapeDtypeStruct((faces, extent), jnp.int32), f32(faces, extent), f32(faces, extent),
        ),
        in_specs=[VMEM] * 6,
        out_specs=(VMEM,) * 6,
        compiler_params=params,
    )(
        starting_motion[0], start_traction[0], load_response[0], orientation[0],
        stiffness.reshape(faces, extent), history.reshape(faces, extent),
    )

    def ascent_of(side, begin, other):
        return pl.pallas_call(
            functools.partial(linear_section, side),
            out_shape=f32(group, times + SUBLANES if begin else times, extent),
            in_specs=[SMEM, SMEM] + [VMEM] * 7,
            out_specs=VMEM,
            scratch_shapes=[pltpu.VMEM((rows * faces, times, extent), jnp.bfloat16)],
            compiler_params=params,
        )(columns, place, compliance, half, other, robin, load, stiff, record)

    for iteration in range(ITERS):
        begin, last = iteration == 0, iteration == ITERS - 1
        other = lax.ppermute(half, "row", swap)
        ascent_far = ascent_of(1, begin, other)
        mates_far = lax.ppermute(ascent_far, "sub", far_pairs)
        ascent_near = ascent_of(0, begin, other)
        mates_near = lax.ppermute(ascent_near, "sub", near_pairs)
        outs = (bf16(times, faces * extent),) * 2 if last else (f32(*tall), bf16(*tall))
        if begin:
            outs += (f32(faces, extent),) * 2
        robin, half, *pair = pl.pallas_call(
            functools.partial(local_section, begin, last),
            out_shape=outs,
            in_specs=[SMEM, SMEM] + [VMEM] * 7,
            out_specs=(VMEM,) * len(outs),
            compiler_params=params,
        )(place, partner, turn, ascent_near, ascent_far, mates_near, mates_far, stiff, record)
        if begin:
            stiff, record = pair
    return robin[None], half[None]


def solution(mesh):
    in_specs = (
        P("sub", "row", None, None, None),
        P("sub", "row", None),
        P("sub", None, "row"),
        P("sub", None, "row"),
        P("sub", None, "row"),
        P("sub", "row"),
        P("sub", "row"),
        P("sub", "row"),
        P("sub", "row", None),
    )
    out_specs = (P("sub", None, "row"), P("sub", None, "row"))
    return jax.shard_map(shards, mesh=mesh, in_specs=in_specs, out_specs=out_specs, check_vma=False)
```

time: 199 us -> 72.3 us (0.36)
  the two profiles are of different devices: /device:TPU:13 before, /device:TPU:9 now
where the time goes in v1:
time: 72.3 us; the launch traced here: 71.8 us
  waiting for transfers between devices  27.7 us (38%)
  Pallas kernels  19 us (26%)
  starting transfers between devices  14.7 us (20%)
  local copies, waits for them, and re-layouts  8.17 us (11%)
  other arithmetic  1.54 us (2%)
  between operations  0.73 us (1%)
    ppermute x3, waiting for transfers between devices, shards(): mates_far = lax.ppermute(ascent_far, 'sub', far_pairs)  16.6 us
    pallas_call x6, Pallas kernels, ascent_of(): pl.pallas_call(functools.partial(linear_section, side), out_shape=f32(gro...  15.4 us
    ppermute x3, waiting for transfers between devices, shards(): other = lax.ppermute(half, 'row', swap)  11.1 us
    ppermute x3, starting transfers between devices, shards(): mates_far = lax.ppermute(ascent_far, 'sub', far_pairs)  8.32 us
    unnamed x18, local copies, waits for them, and re-layouts  8.17 us
    ppermute x3, starting transfers between devices, shards(): other = lax.ppermute(half, 'row', swap)  3.82 us
    pallas_call x3, Pallas kernels, shards(): pl.pallas_call(functools.partial(local_section, begin, last), out_shape=o...  3.52 us
    ppermute x3, starting transfers between devices, shards(): mates_near = lax.ppermute(ascent_near, 'sub', near_pairs)  2.54 us
  transfers between devices with their start and end apart: 9, of which 6 were waited for; matrix products, arithmetic and copies ran while one was open for 1% of the time, Pallas kernels for 11%

profile of v1, /device:TPU:9, one launch (start us, length us, event | category | flops | bytes accessed | tf_op | source)
XLA Modules:
  0.0 71.8 jit_solution(14303401988671288485)
XLA Ops:
  0.6 0.7 %reduce = f32[2304]{0:T(1024)S(1)} reduce(f32[1,2304]{1,0:T(1,128)} %param.14, f32[]{:T(128)} %constant.32), dimensions={0}, to_apply=%param.14.reduce_sub_computation | reduce | bytes 18436 | tf_op args[5]
  1.4 0.7 %reduce.1 = f32[2304]{0:T(1024)S(1)} reduce(f32[1,2304]{1,0:T(1,128)} %param.15, f32[]{:T(128)} %constant.32), dimensions={0}, to_apply=%param.15.reduce_sub_computation | reduce | bytes 18436 | tf_op args[6]
  2.1 0.7 copy.16
  2.8 0.9 %copy-done.1 = bf16[1,32,2304]{2,1,0:T(8,128)(2,1)S(1)} copy-done((bf16[1,32,2304]{2,1,0:T(8,128)(2,1)S(1)}, bf16[1,32,2304]{2,1,0:T(8,128)(2,1)}, u32[]{:S(2)}) %copy-start.1) | copy-done | bytes 147480
  3.7 0.9 %copy-done.2 = bf16[1,32,2304]{2,1,0:T(8,128)(2,1)S(1)} copy-done((bf16[1,32,2304]{2,1,0:T(8,128)(2,1)S(1)}, bf16[1,32,2304]{2,1,0:T(8,128)(2,1)}, u32[]{:S(2)}) %copy-start.2) | copy-done | bytes 147480
  4.6 0.9 %copy-done.3 = bf16[1,32,2304]{2,1,0:T(8,128)(2,1)S(1)} copy-done((bf16[1,32,2304]{2,1,0:T(8,128)(2,1)S(1)}, bf16[1,32,2304]{2,1,0:T(8,128)(2,1)}, u32[]{:S(2)}) %copy-start.3) | copy-done | bytes 147480
  5.6 1.3 %collective-permute-start = (bf16[18,32,128]{2,1,0:T(8,128)(2,1)S(1)}, bf16[18,32,128]{2,1,0:T(8,128)(2,1)S(1)}, u32[]{:S(2)}, u32[]{:S(2)}) collective-permute-start(bf16[18,32,128]{2,1,0:T(8,128)(2,1)S(1)} %get-tuple-element.17.own_ref), channel_id=1, source_target_pairs={{0,1},{1,0},{2,3},{3,2},{4,5},{5,4},{6,7},{7,6},{8,9},{9,8},{10,11... | collective-permute-start | bytes 442376 | tf_op jit(solution)/shard_map/ppermute | solution.py:165
  6.9 0.7 copy.15
  7.6 2.7 %collective-permute-done.other_ref = bf16[18,32,128]{2,1,0:T(8,128)(2,1)S(1)} collective-permute-done((bf16[18,32,128]{2,1,0:T(8,128)(2,1)S(1)}, bf16[18,32,128]{2,1,0:T(8,128)(2,1)S(1)}, u32[]{:S(2)}, u32[]{:S(2)}) %collective-permute-start) | collective-permute-done | bytes 147488 | tf_op jit(solution)/shard_map/ppermute | solution.py:165
  10.4 4.0 %copy-done = bf16[1,18,18,128,128]{4,3,2,1,0:T(8,128)(2,1)S(1)} copy-done((bf16[1,18,18,128,128]{4,3,2,1,0:T(8,128)(2,1)S(1)}, bf16[1,18,18,128,128]{4,3,2,1,0:T(8,128)(2,1)}, u32[]{:S(2)}) %copy-start) | copy-done | bytes 10616856
  14.4 2.6 %shard_map.105.own0_ref = f32[9,40,128]{2,1,0:T(8,128)S(1)} custom-call(s32[18,18]{1,0:T(8,128)S(1)} %bitcast.26, s32[3]{0:T(128)S(1)} %pad_add_fusion.place_ref, bf16[18,18,128,128]{3,2,1,0:T(8,128)(2,1)S(1)} %bitcast.18, bf16[18,32,128]{2,1,0:T(8,128)(2,1)S(1)} %get-tuple-element.17.own_ref, bf16[18,32,128]{2,1,0:T(8,128)(2,1)S(1)} %collective-permute-done.other_ref, ...), custom_call_target="tpu_custom_call" | custom-call | tf_op jit(solution)/shard_map/pallas_call | solution.py:154
  17.0 1.6 %collective-permute-start.1 = (f32[9,40,128]{2,1,0:T(8,128)S(1)}, f32[9,40,128]{2,1,0:T(8,128)S(1)}, u32[]{:S(2)}, u32[]{:S(2)}) collective-permute-start(f32[9,40,128]{2,1,0:T(8,128)S(1)} %shard_map.105.own0_ref), channel_id=1, source_target_pairs={{0,2},{2,0},{4,6},{6,4},{8,10},{10,8},{12,14},{14,12},{16,18},{18,... | collective-permute-start | bytes 552968 | tf_op jit(solution)/shard_map/ppermute | solution.py:169
  18.6 2.6 %shard_map.106.own1_ref = f32[9,40,128]{2,1,0:T(8,128)S(1)} custom-call(s32[18,18]{1,0:T(8,128)S(1)} %bitcast.27, s32[3]{0:T(128)S(1)} %pad_add_fusion.place_ref, bf16[18,18,128,128]{3,2,1,0:T(8,128)(2,1)S(1)} %bitcast.19, bf16[18,32,128]{2,1,0:T(8,128)(2,1)S(1)} %get-tuple-element.17.own_ref, bf16[18,32,128]{2,1,0:T(8,128)(2,1)S(1)} %collective-permute-done.other_ref, ...), custom_call_target="tpu_custom_call" | custom-call | tf_op jit(solution)/shard_map/pallas_call | solution.py:154
  21.2 3.1 %collective-permute-start.2 = (f32[9,40,128]{2,1,0:T(8,128)S(1)}, f32[9,40,128]{2,1,0:T(8,128)S(1)}, u32[]{:S(2)}, u32[]{:S(2)}) collective-permute-start(f32[9,40,128]{2,1,0:T(8,128)S(1)} %shard_map.106.own1_ref), channel_id=1, source_target_pairs={{2,4},{4,2},{6,8},{8,6},{10,12},{12,10},{14,16},{16,14},{18,20},{2... | collective-permute-start | bytes 552968 | tf_op jit(solution)/shard_map/ppermute | solution.py:167
  24.2 5.8 %collective-permute-done.2.mate1_ref = f32[9,40,128]{2,1,0:T(8,128)S(1)} collective-permute-done((f32[9,40,128]{2,1,0:T(8,128)S(1)}, f32[9,40,128]{2,1,0:T(8,128)S(1)}, u32[]{:S(2)}, u32[]{:S(2)}) %collective-permute-start.2) | collective-permute-done | bytes 184352 | tf_op jit(solution)/shard_map/ppermute | solution.py:167
  30.0 1.0 %shard_map.107 = (f32[18,32,128]{2,1,0:T(8,128)S(1)}, bf16[18,32,128]{2,1,0:T(8,128)(2,1)S(1)}, f32[18,128]{1,0:T(8,128)S(1)}, f32[18,128]{1,0:T(8,128)S(1)}) custom-call(s32[3]{0:T(128)S(1)} %pad_add_fusion.place_ref, s32[18]{0:T(128)S(1)} %bitcast.38, s32[18,128]{1,0:T(8,128)S(1)} %get-tuple-element.16.turn_ref, f32[9,40,128]{2,1,0:T(8,128)S(1)} %shard_map.105.own0_ref, ...), custom_call_target="tpu_custom_call" | custom-call | tf_op jit(solution)/shard_map/pallas_call | solution.py:173
  31.0 1.3 %collective-permute-start.3 = (bf16[18,32,128]{2,1,0:T(8,128)(2,1)S(1)}, bf16[18,32,128]{2,1,0:T(8,128)(2,1)S(1)}, u32[]{:S(2)}, u32[]{:S(2)}) collective-permute-start(bf16[18,32,128]{2,1,0:T(8,128)(2,1)S(1)} %get-tuple-element.22.own_ref), channel_id=1, source_target_pairs={{0,1},{1,0},{2,3},{3,2},{4,5},{5,4},{6,7},{7,6},{8,9},{9,8},{10,11... | collective-permute-start | bytes 442376 | tf_op jit(solution)/shard_map/ppermute | solution.py:165
  32.2 3.9 %collective-permute-done.3.other_ref = bf16[18,32,128]{2,1,0:T(8,128)(2,1)S(1)} collective-permute-done((bf16[18,32,128]{2,1,0:T(8,128)(2,1)S(1)}, bf16[18,32,128]{2,1,0:T(8,128)(2,1)S(1)}, u32[]{:S(2)}, u32[]{:S(2)}) %collective-permute-start.3) | collective-permute-done | bytes 147488 | tf_op jit(solution)/shard_map/ppermute | solution.py:165
  36.1 2.6 %shard_map.108.own0_ref = f32[9,32,128]{2,1,0:T(8,128)S(1)} custom-call(s32[18,18]{1,0:T(8,128)S(1)} %bitcast.28, s32[3]{0:T(128)S(1)} %pad_add_fusion.place_ref, bf16[18,18,128,128]{3,2,1,0:T(8,128)(2,1)S(1)} %bitcast.22, bf16[18,32,128]{2,1,0:T(8,128)(2,1)S(1)} %get-tuple-element.22.own_ref, bf16[18,32,128]{2,1,0:T(8,128)(2,1)S(1)} %collective-permute-done.3.other_ref, ...), custom_call_target="tpu_custom_call" | custom-call | tf_op jit(solution)/shard_map/pallas_call | solution.py:154
  38.7 0.3 collective-permute-start.4
  39.1 2.6 %shard_map.109.own1_ref = f32[9,32,128]{2,1,0:T(8,128)S(1)} custom-call(s32[18,18]{1,0:T(8,128)S(1)} %bitcast.29, s32[3]{0:T(128)S(1)} %pad_add_fusion.place_ref, bf16[18,18,128,128]{3,2,1,0:T(8,128)(2,1)S(1)} %bitcast.23, bf16[18,32,128]{2,1,0:T(8,128)(2,1)S(1)} %get-tuple-element.22.own_ref, bf16[18,32,128]{2,1,0:T(8,128)(2,1)S(1)} %collective-permute-done.3.other_ref, ...), custom_call_target="tpu_custom_call" | custom-call | tf_op jit(solution)/shard_map/pallas_call | solution.py:154
  41.6 3.0 %collective-permute-start.5 = (f32[9,32,128]{2,1,0:T(8,128)S(1)}, f32[9,32,128]{2,1,0:T(8,128)S(1)}, u32[]{:S(2)}, u32[]{:S(2)}) collective-permute-start(f32[9,32,128]{2,1,0:T(8,128)S(1)} %shard_map.109.own1_ref), channel_id=1, source_target_pairs={{2,4},{4,2},{6,8},{8,6},{10,12},{12,10},{14,16},{16,14},{18,20},{2... | collective-permute-start | bytes 442376 | tf_op jit(solution)/shard_map/ppermute | solution.py:167
  44.6 5.0 %collective-permute-done.5.mate1_ref = f32[9,32,128]{2,1,0:T(8,128)S(1)} collective-permute-done((f32[9,32,128]{2,1,0:T(8,128)S(1)}, f32[9,32,128]{2,1,0:T(8,128)S(1)}, u32[]{:S(2)}, u32[]{:S(2)}) %collective-permute-start.5) | collective-permute-done | bytes 147488 | tf_op jit(solution)/shard_map/ppermute | solution.py:167
  49.7 0.9 %shard_map.110 = (f32[18,32,128]{2,1,0:T(8,128)S(1)}, bf16[18,32,128]{2,1,0:T(8,128)(2,1)S(1)}) custom-call(s32[3]{0:T(128)S(1)} %pad_add_fusion.place_ref, s32[18]{0:T(128)S(1)} %bitcast.39, s32[18,128]{1,0:T(8,128)S(1)} %get-tuple-element.16.turn_ref, f32[9,32,128]{2,1,0:T(8,128)S(1)} %shard_map.108.own0_ref, f32[9,32,128]{2,1,0:T(8,128)S(1)} %shard_map.109.own1_ref, ...), custom_call_target="tpu_custom_call" | custom-call | tf_op jit(solution)/shard_map/pallas_call | solution.py:173
  50.6 1.3 %collective-permute-start.6 = (bf16[18,32,128]{2,1,0:T(8,128)(2,1)S(1)}, bf16[18,32,128]{2,1,0:T(8,128)(2,1)S(1)}, u32[]{:S(2)}, u32[]{:S(2)}) collective-permute-start(bf16[18,32,128]{2,1,0:T(8,128)(2,1)S(1)} %get-tuple-element.26.own_ref), channel_id=1, source_target_pairs={{0,1},{1,0},{2,3},{3,2},{4,5},{5,4},{6,7},{7,6},{8,9},{9,8},{10,11... | collective-permute-start | bytes 442376 | tf_op jit(solution)/shard_map/ppermute | solution.py:165
  51.9 4.5 %collective-permute-done.6.other_ref = bf16[18,32,128]{2,1,0:T(8,128)(2,1)S(1)} collective-permute-done((bf16[18,32,128]{2,1,0:T(8,128)(2,1)S(1)}, bf16[18,32,128]{2,1,0:T(8,128)(2,1)S(1)}, u32[]{:S(2)}, u32[]{:S(2)}) %collective-permute-start.6) | collective-permute-done | bytes 147488 | tf_op jit(solution)/shard_map/ppermute | solution.py:165
  56.4 2.6 %shard_map.111.own0_ref = f32[9,32,128]{2,1,0:T(8,128)S(1)} custom-call(s32[18,18]{1,0:T(8,128)S(1)} %bitcast.30, s32[3]{0:T(128)S(1)} %pad_add_fusion.place_ref, bf16[18,18,128,128]{3,2,1,0:T(8,128)(2,1)S(1)} %bitcast.24, bf16[18,32,128]{2,1,0:T(8,128)(2,1)S(1)} %get-tuple-element.26.own_ref, bf16[18,32,128]{2,1,0:T(8,128)(2,1)S(1)} %collective-permute-done.6.other_ref, ...), custom_call_target="tpu_custom_call" | custom-call | tf_op jit(solution)/shard_map/pallas_call | solution.py:154
  59.0 0.6 collective-permute-start.7
  59.6 2.6 %shard_map.112.own1_ref = f32[9,32,128]{2,1,0:T(8,128)S(1)} custom-call(s32[18,18]{1,0:T(8,128)S(1)} %bitcast.31, s32[3]{0:T(128)S(1)} %pad_add_fusion.place_ref, bf16[18,18,128,128]{3,2,1,0:T(8,128)(2,1)S(1)} %bitcast.25, bf16[18,32,128]{2,1,0:T(8,128)(2,1)S(1)} %get-tuple-element.26.own_ref, bf16[18,32,128]{2,1,0:T(8,128)(2,1)S(1)} %collective-permute-done.6.other_ref, ...), custom_call_target="tpu_custom_call" | custom-call | tf_op jit(solution)/shard_map/pallas_call | solution.py:154
  62.1 2.3 %collective-permute-start.8 = (f32[9,32,128]{2,1,0:T(8,128)S(1)}, f32[9,32,128]{2,1,0:T(8,128)S(1)}, u32[]{:S(2)}, u32[]{:S(2)}) collective-permute-start(f32[9,32,128]{2,1,0:T(8,128)S(1)} %shard_map.112.own1_ref), channel_id=1, source_target_pairs={{2,4},{4,2},{6,8},{8,6},{10,12},{12,10},{14,16},{16,14},{18,20},{2... | collective-permute-start | bytes 442376 | tf_op jit(solution)/shard_map/ppermute | solution.py:167
  64.4 5.8 %collective-permute-done.8.mate1_ref = f32[9,32,128]{2,1,0:T(8,128)S(1)} collective-permute-done((f32[9,32,128]{2,1,0:T(8,128)S(1)}, f32[9,32,128]{2,1,0:T(8,128)S(1)}, u32[]{:S(2)}, u32[]{:S(2)}) %collective-permute-start.8) | collective-permute-done | bytes 147488 | tf_op jit(solution)/shard_map/ppermute | solution.py:167
  70.2 1.6 %shard_map.113 = (bf16[32,2304]{1,0:T(8,128)(2,1)}, bf16[32,2304]{1,0:T(8,128)(2,1)}) custom-call(s32[3]{0:T(128)S(1)} %pad_add_fusion.place_ref, s32[18]{0:T(128)S(1)} %bitcast.40, s32[18,128]{1,0:T(8,128)S(1)} %get-tuple-element.16.turn_ref, f32[9,32,128]{2,1,0:T(8,128)S(1)} %shard_map.111.own0_ref, f32[9,32,128]{2,1,0:T(8,128)S(1)} %shard_map.112.own1_ref, ...), custom_call_target="tpu_custom_call" | custom-call | tf_op jit(solution)/shard_map/pallas_call | solution.py:173
  (18 shorter events, 0.2 us)
Async XLA Ops:
  2.8 0.9 %copy-start.1 = (bf16[1,32,2304]{2,1,0:T(8,128)(2,1)S(1)}, bf16[1,32,2304]{2,1,0:T(8,128)(2,1)}, u32[]{:S(2)}) copy-start(bf16[1,32,2304]{2,1,0:T(8,128)(2,1)} %param.12) | copy-start | bytes 442372
  3.7 0.9 %copy-start.2 = (bf16[1,32,2304]{2,1,0:T(8,128)(2,1)S(1)}, bf16[1,32,2304]{2,1,0:T(8,128)(2,1)}, u32[]{:S(2)}) copy-start(bf16[1,32,2304]{2,1,0:T(8,128)(2,1)} %param.13) | copy-start | bytes 442372
  4.6 0.9 %copy-start.3 = (bf16[1,32,2304]{2,1,0:T(8,128)(2,1)S(1)}, bf16[1,32,2304]{2,1,0:T(8,128)(2,1)}, u32[]{:S(2)}) copy-start(bf16[1,32,2304]{2,1,0:T(8,128)(2,1)} %param.11) | copy-start | bytes 442372
  5.6 4.8 %collective-permute-start = (bf16[18,32,128]{2,1,0:T(8,128)(2,1)S(1)}, bf16[18,32,128]{2,1,0:T(8,128)(2,1)S(1)}, u32[]{:S(2)}, u32[]{:S(2)}) collective-permute-start(bf16[18,32,128]{2,1,0:T(8,128)(2,1)S(1)} %get-tuple-element.17.own_ref), channel_id=1, source_target_pairs={{0,1},{1,0},{2,3},{3,2},{4,5},{5,4},{6,7},{7,6},{8,9},{9,8},{10,11... | collective-permute-start | bytes 442376 | tf_op jit(solution)/shard_map/ppermute | solution.py:165
  10.4 4.0 %copy-start = (bf16[1,18,18,128,128]{4,3,2,1,0:T(8,128)(2,1)S(1)}, bf16[1,18,18,128,128]{4,3,2,1,0:T(8,128)(2,1)}, u32[]{:S(2)}) copy-start(bf16[1,18,18,128,128]{4,3,2,1,0:T(8,128)(2,1)} %param.9) | copy-start | bytes 31850500
  14.4 15.6 %copy-start.4 = (s32[1,18]{1,0:T(1,128)S(1)}, s32[1,18]{1,0:T(1,128)}, u32[]{:S(2)}) copy-start(s32[1,18]{1,0:T(1,128)} %param.16) | copy-start | bytes 220
  14.4 21.7 %slice-start = ((s8[10616832]{0:T(1024)(128)(4,1)}), s8[4194304]{0:T(1024)(128)(4,1)S(1)}, s32[]{:S(2)}) async-start(s8[10616832]{0:T(1024)(128)(4,1)} %bitcast.20), calls=%async_computation | async-start | bytes 8388608
  14.4 21.7 %slice-start.1 = ((s8[10616832]{0:T(1024)(128)(4,1)}), s8[4194304]{0:T(1024)(128)(4,1)S(1)}, s32[]{:S(2)}) async-start(s8[10616832]{0:T(1024)(128)(4,1)} %bitcast.20), calls=%async_computation.1 | async-start | bytes 8388608
  17.0 19.2 %slice-start.2 = ((s8[10616832]{0:T(1024)(128)(4,1)}), s8[2228224]{0:T(1024)(128)(4,1)S(1)}, s32[]{:S(2)}) async-start(s8[10616832]{0:T(1024)(128)(4,1)} %bitcast.20), calls=%async_computation.2 | async-start | bytes 4456448
  17.0 7.3 %collective-permute-start.1 = (f32[9,40,128]{2,1,0:T(8,128)S(1)}, f32[9,40,128]{2,1,0:T(8,128)S(1)}, u32[]{:S(2)}, u32[]{:S(2)}) collective-permute-start(f32[9,40,128]{2,1,0:T(8,128)S(1)} %shard_map.105.own0_ref), channel_id=1, source_target_pairs={{0,2},{2,0},{4,6},{6,4},{8,10},{10,8},{12,14},{14,12},{16,18},{18,... | collective-permute-start | bytes 552968 | tf_op jit(solution)/shard_map/ppermute | solution.py:169
  21.2 8.8 %collective-permute-start.2 = (f32[9,40,128]{2,1,0:T(8,128)S(1)}, f32[9,40,128]{2,1,0:T(8,128)S(1)}, u32[]{:S(2)}, u32[]{:S(2)}) collective-permute-start(f32[9,40,128]{2,1,0:T(8,128)S(1)} %shard_map.106.own1_ref), channel_id=1, source_target_pairs={{2,4},{4,2},{6,8},{8,6},{10,12},{12,10},{14,16},{16,14},{18,20},{2... | collective-permute-start | bytes 552968 | tf_op jit(solution)/shard_map/ppermute | solution.py:167
  31.0 5.2 %collective-permute-start.3 = (bf16[18,32,128]{2,1,0:T(8,128)(2,1)S(1)}, bf16[18,32,128]{2,1,0:T(8,128)(2,1)S(1)}, u32[]{:S(2)}, u32[]{:S(2)}) collective-permute-start(bf16[18,32,128]{2,1,0:T(8,128)(2,1)S(1)} %get-tuple-element.22.own_ref), channel_id=1, source_target_pairs={{0,1},{1,0},{2,3},{3,2},{4,5},{5,4},{6,7},{7,6},{8,9},{9,8},{10,11... | collective-permute-start | bytes 442376 | tf_op jit(solution)/shard_map/ppermute | solution.py:165
  38.7 5.9 %collective-permute-start.4 = (f32[9,32,128]{2,1,0:T(8,128)S(1)}, f32[9,32,128]{2,1,0:T(8,128)S(1)}, u32[]{:S(2)}, u32[]{:S(2)}) collective-permute-start(f32[9,32,128]{2,1,0:T(8,128)S(1)} %shard_map.108.own0_ref), channel_id=1, source_target_pairs={{0,2},{2,0},{4,6},{6,4},{8,10},{10,8},{12,14},{14,12},{16,18},{18,... | collective-permute-start | bytes 442376 | tf_op jit(solution)/shard_map/ppermute | solution.py:169
  41.6 8.1 %collective-permute-start.5 = (f32[9,32,128]{2,1,0:T(8,128)S(1)}, f32[9,32,128]{2,1,0:T(8,128)S(1)}, u32[]{:S(2)}, u32[]{:S(2)}) collective-permute-start(f32[9,32,128]{2,1,0:T(8,128)S(1)} %shard_map.109.own1_ref), channel_id=1, source_target_pairs={{2,4},{4,2},{6,8},{8,6},{10,12},{12,10},{14,16},{16,14},{18,20},{2... | collective-permute-start | bytes 442376 | tf_op jit(solution)/shard_map/ppermute | solution.py:167
  50.6 5.8 %collective-permute-start.6 = (bf16[18,32,128]{2,1,0:T(8,128)(2,1)S(1)}, bf16[18,32,128]{2,1,0:T(8,128)(2,1)S(1)}, u32[]{:S(2)}, u32[]{:S(2)}) collective-permute-start(bf16[18,32,128]{2,1,0:T(8,128)(2,1)S(1)} %get-tuple-element.26.own_ref), channel_id=1, source_target_pairs={{0,1},{1,0},{2,3},{3,2},{4,5},{5,4},{6,7},{7,6},{8,9},{9,8},{10,11... | collective-permute-start | bytes 442376 | tf_op jit(solution)/shard_map/ppermute | solution.py:165
  59.0 5.4 %collective-permute-start.7 = (f32[9,32,128]{2,1,0:T(8,128)S(1)}, f32[9,32,128]{2,1,0:T(8,128)S(1)}, u32[]{:S(2)}, u32[]{:S(2)}) collective-permute-start(f32[9,32,128]{2,1,0:T(8,128)S(1)} %shard_map.111.own0_ref), channel_id=1, source_target_pairs={{0,2},{2,0},{4,6},{6,4},{8,10},{10,8},{12,14},{14,12},{16,18},{18,... | collective-permute-start | bytes 442376 | tf_op jit(solution)/shard_map/ppermute | solution.py:169
  62.1 8.1 %collective-permute-start.8 = (f32[9,32,128]{2,1,0:T(8,128)S(1)}, f32[9,32,128]{2,1,0:T(8,128)S(1)}, u32[]{:S(2)}, u32[]{:S(2)}) collective-permute-start(f32[9,32,128]{2,1,0:T(8,128)S(1)} %shard_map.112.own1_ref), channel_id=1, source_target_pairs={{2,4},{4,2},{6,8},{8,6},{10,12},{12,10},{14,16},{16,14},{18,20},{2... | collective-permute-start | bytes 442376 | tf_op jit(solution)/shard_map/ppermute | solution.py:167

commit v2 on v1

v2 whole, which is shorter than its diff:
```python
import functools

import jax
import jax.numpy as jnp
from jax import lax
from jax.experimental import pallas as pl
from jax.experimental.pallas import tpu as pltpu
from jax.sharding import PartitionSpec as P

ITERS = 3
SUBLANES = 8
VMEM_BYTES = 24 * 2**20

ONSET_JUMP = 0.15
FAILURE_JUMP = 1.5

VMEM = pl.BlockSpec(memory_space=pltpu.VMEM)
SMEM = pl.BlockSpec(memory_space=pltpu.SMEM)
ANY = pl.BlockSpec(memory_space=pl.ANY)


def position(group):
    near = group * (lax.axis_index("sub") % 2)
    return near, group - near, lax.axis_index("row")


def first_robin(motion_hbm, stress_hbm, robin_ref, half_ref, motion_ref, stress_ref, sems):
    copies = [
        pltpu.make_async_copy(motion_hbm, motion_ref, sems.at[0]),
        pltpu.make_async_copy(stress_hbm, stress_ref, sems.at[1]),
    ]
    for copy in copies:
        copy.start()
    for copy in copies:
        copy.wait()
    faces, _, extent = robin_ref.shape
    for face in range(faces):
        lanes = slice(face * extent, (face + 1) * extent)
        robin = stress_ref[:, lanes].astype(jnp.float32) + motion_ref[:, lanes].astype(jnp.float32)
        robin_ref[face] = robin
        half_ref[face] = robin.astype(jnp.bfloat16)


def block_products(parts):
    times, extent = parts[0][0][0].shape
    zero = jnp.zeros_like(parts[0][0][1])
    depth = max(len(part) for part in parts)
    parts = [part + [(part[0][0], zero)] * (depth - len(part)) for part in parts]
    values = jnp.concatenate([jnp.concatenate([v for v, _ in part], axis=1) for part in parts], axis=0)
    blocks = jnp.concatenate([jnp.concatenate([c for _, c in part], axis=1) for part in parts], axis=0)
    product = lax.dot_general(values, blocks, (((1,), (1,)), ((), ())), preferred_element_type=jnp.float32)
    return [
        product[p * times : (p + 1) * times, p * extent : (p + 1) * extent] for p in range(len(parts))
    ]


def linear_section(side, columns_ref, compliance_ref, own_ref, other_ref, robin_ref, load_ref,
                   stiff_ref, record_ref, *refs):
    out_ref, half_ref = refs[-2:]
    group, rows, extent = out_ref.shape
    faces, times, _ = own_ref.shape
    stored = compliance_ref.shape[1]
    *starts, mine = position(group)
    first = starts[side]
    half_ref[pl.ds(mine * faces, faces)] = own_ref[...]
    half_ref[pl.ds((1 - mine) * faces, faces)] = other_ref[...]

    def entries(face, begin, end):
        return [(half_ref[columns_ref[face, 0, j]], compliance_ref[face, j]) for j in range(begin, end)]

    def finish(index, product):
        face = first + index
        lanes = pl.ds(pl.multiple_of(face * extent, extent), extent)
        response = product + load_ref[:, lanes].astype(jnp.float32)
        out_ref[index, :times] = robin_ref[face] - 2.0 * response
        if rows > times:
            out_ref[index, times : times + 1] = stiff_ref[:, lanes]
            out_ref[index, times + 1 : times + 2] = record_ref[:, lanes]
            out_ref[index, times + 2 :] = jnp.zeros_like(out_ref[index, times + 2 :])

    for index in range(0, group - 1, 2):
        pair = block_products([entries(first + index + k, 0, stored) for k in range(2)])
        for k in range(2):
            finish(index + k, pair[k])
    if group % 2:
        face = first + group - 1
        cut = (stored + 3) // 4 * 2
        finish(group - 1, sum(block_products([entries(face, 0, cut), entries(face, cut, stored)])))


def running_peak(sizes):
    row = lax.broadcasted_iota(jnp.int32, sizes.shape, 0)
    step = 1
    while step < sizes.shape[0]:
        earlier = pltpu.roll(sizes, step, 0)
        sizes = jnp.maximum(sizes, jnp.where(row >= step, earlier, 0.0))
        step *= 2
    return sizes


def local_section(begin, last, partner_ref, turn_ref, own0_ref, own1_ref, mate0_ref, mate1_ref,
                  stiff_ref, record_ref, first_ref, second_ref, *pair_refs):
    group = own0_ref.shape[0]
    extent = own0_ref.shape[2]
    times = first_ref.shape[0] if last else first_ref.shape[1]
    starts = position(group)
    gather = functools.partial(jnp.take_along_axis, axis=1, mode="promise_in_bounds")
    for side, (own_ref, mate_ref) in enumerate(((own0_ref, mate0_ref), (own1_ref, mate1_ref))):
        for index in range(group):
            face = starts[side] + index
            lanes = pl.ds(pl.multiple_of(face * extent, extent), extent)
            partner = partner_ref[0, face]
            mate = jnp.maximum(partner, 0)
            turn = turn_ref[:, lanes]
            ascent = own_ref[index, :times]
            mate_ascent = gather(mate_ref[mate, :times], jnp.broadcast_to(turn, (times, extent)))
            stiffness = stiff_ref[:, lanes]
            record = record_ref[:, lanes]
            if begin:
                constants = gather(mate_ref[mate, times:], jnp.broadcast_to(turn, (SUBLANES, extent)))
                stiffness = 0.5 * (stiffness + constants[:1])
                record = jnp.maximum(record, constants[1:2])
                pair_refs[0][:, lanes] = stiffness
                pair_refs[1][:, lanes] = record
            difference = ascent - mate_ascent
            jump = difference / (1.0 + 2.0 * stiffness)
            peak = jnp.maximum(record, running_peak(jnp.abs(jump)))
            damage = jnp.clip((peak - ONSET_JUMP) / (FAILURE_JUMP - ONSET_JUMP), 0.0, 1.0)
            effective = stiffness * (1.0 - damage)
            traction = jnp.where(partner >= 0, effective * difference / (1.0 + 2.0 * effective), 0.0)
            motion = traction - ascent
            if last:
                first_ref[:, lanes] = motion.astype(jnp.bfloat16)
                second_ref[:, lanes] = traction.astype(jnp.bfloat16)
            else:
                robin = traction + motion
                first_ref[face] = robin
                second_ref[face] = robin.astype(jnp.bfloat16)


def shards(
    compliance,
    block_columns,
    load_response,
    starting_motion,
    start_traction,
    stiffness,
    history,
    face_partner,
    orientation,
):
    _, faces, stored, extent, _ = compliance.shape
    times = starting_motion.shape[1]
    group = faces // 2
    subs = lax.axis_size("sub")
    rows = lax.axis_size("row")
    near_pairs = [(s, s ^ 1) for s in range(subs) if s ^ 1 < subs]
    far_pairs = [(s, t) for s in range(subs) for t in [s - 1 if s % 2 == 0 else s + 1] if 0 <= t < subs]
    swap = [(r, rows - 1 - r) for r in range(rows)]
    params = pltpu.CompilerParams(vmem_limit_bytes=VMEM_BYTES)

    compliance = pltpu.with_memory_space_constraint(compliance[0], pltpu.VMEM)
    columns = jnp.transpose(block_columns, (1, 0, 2))
    turn = orientation.reshape(1, -1)
    load = load_response[0]

    def f32(*shape):
        return jax.ShapeDtypeStruct(shape, jnp.float32)

    def bf16(*shape):
        return jax.ShapeDtypeStruct(shape, jnp.bfloat16)

    tall = (faces, times, extent)
    flat = (times, faces * extent)
    robin, half = pl.pallas_call(
        first_robin,
        out_shape=(f32(*tall), bf16(*tall)),
        in_specs=[ANY] * 2,
        out_specs=(VMEM,) * 2,
        scratch_shapes=[
            pltpu.VMEM(flat, jnp.bfloat16), pltpu.VMEM(flat, jnp.bfloat16), pltpu.SemaphoreType.DMA((2,)),
        ],
        compiler_params=params,
    )(starting_motion[0], start_traction[0])

    def ascent_of(side, begin, other, after=()):
        return pl.pallas_call(
            functools.partial(linear_section, side),
            out_shape=f32(group, times + SUBLANES if begin else times, extent),
            in_specs=[SMEM] + [VMEM] * 7 + [ANY] * len(after),
            out_specs=VMEM,
            scratch_shapes=[pltpu.VMEM((rows * faces, times, extent), jnp.bfloat16)],
            compiler_params=params,
        )(columns, compliance, half, other, robin, load, stiffness, history, *after)

    stiff, record = stiffness, history
    for iteration in range(ITERS):
        begin, last = iteration == 0, iteration == ITERS - 1
        other = lax.ppermute(half, "row", swap)
        ascent_far = ascent_of(1, begin, other)
        mates_far = lax.ppermute(ascent_far, "sub", far_pairs)
        ascent_near = ascent_of(0, begin, other, (ascent_far,))
        mates_near = lax.ppermute(ascent_near, "sub", near_pairs)
        outs = (bf16(*flat),) * 2 if last else (f32(*tall), bf16(*tall))
        if begin:
            outs += (f32(1, faces * extent),) * 2
        robin, half, *pair = pl.pallas_call(
            functools.partial(local_section, begin, last),
            out_shape=outs,
            in_specs=[SMEM] + [VMEM] * 7,
            out_specs=(VMEM,) * len(outs),
            compiler_params=params,
        )(face_partner, turn, ascent_near, ascent_far, mates_near, mates_far, stiff, record)
        if begin:
            stiff, record = pair
    return robin[None], half[None]


def solution(mesh):
    in_specs = (
        P("sub", "row", None, None, None),
        P("sub", "row", None),
        P("sub", None, "row"),
        P("sub", None, "row"),
        P("sub", None, "row"),
        P("sub", "row"),
        P("sub", "row"),
        P("sub", "row"),
        P("sub", "row", None),
    )
    out_specs = (P("sub", None, "row"), P("sub", None, "row"))
    return jax.shard_map(shards, mesh=mesh, in_specs=in_specs, out_specs=out_specs, check_vma=False)
```

time: 72.3 us -> 71.8 us (level)
  the two profiles are of different devices: /device:TPU:9 before, /device:TPU:27 now
where the time goes in v2:
time: 71.8 us; the launch traced here: 71.4 us
  waiting for transfers between devices  32.7 us (46%)
  Pallas kernels  18.6 us (26%)
  starting transfers between devices  10.4 us (14%)
  local copies, waits for them, and re-layouts  8.87 us (12%)
  between operations  0.81 us (1%)
    ppermute x3, waiting for transfers between devices, shards(): mates_far = lax.ppermute(ascent_far, 'sub', far_pairs)  18 us
    ppermute x3, waiting for transfers between devices, shards(): other = lax.ppermute(half, 'row', swap)  14.8 us
    pallas_call x6, Pallas kernels, ascent_of(): pl.pallas_call(functools.partial(linear_section, side), out_shape=f32(gro...  14.6 us
    unnamed x26, local copies, waits for them, and re-layouts  8.87 us
    ppermute x3, starting transfers between devices, shards(): mates_far = lax.ppermute(ascent_far, 'sub', far_pairs)  6.87 us
    pallas_call x3, Pallas kernels, shards(): pl.pallas_call(functools.partial(local_section, begin, last), out_shape=o...  3.57 us
    ppermute x3, starting transfers between devices, shards(): mates_near = lax.ppermute(ascent_near, 'sub', near_pairs)  2.55 us
  transfers between devices with their start and end apart: 9, of which 6 were waited for; matrix products, arithmetic and copies ran while one was open for 0% of the time, Pallas kernels for 0%

profile of v2, /device:TPU:27, one launch (start us, length us, event | category | flops | bytes accessed | tf_op | source)
XLA Modules:
  0.0 71.4 jit_solution(16546434221919766464)
XLA Ops:
  0.6 0.9 %copy-done.6 = bf16[1,32,2304]{2,1,0:T(8,128)(2,1)S(1)} copy-done((bf16[1,32,2304]{2,1,0:T(8,128)(2,1)S(1)}, bf16[1,32,2304]{2,1,0:T(8,128)(2,1)}, u32[]{:S(2)}) %copy-start.6) | copy-done | bytes 147480
  1.5 0.9 %copy-done.7 = bf16[1,32,2304]{2,1,0:T(8,128)(2,1)S(1)} copy-done((bf16[1,32,2304]{2,1,0:T(8,128)(2,1)S(1)}, bf16[1,32,2304]{2,1,0:T(8,128)(2,1)}, u32[]{:S(2)}) %copy-start.7) | copy-done | bytes 147480
  2.5 0.4 shard_map.104
  2.9 0.3 collective-permute-start
  3.2 4.5 %collective-permute-done.other_ref = bf16[18,32,128]{2,1,0:T(8,128)(2,1)S(1)} collective-permute-done((bf16[18,32,128]{2,1,0:T(8,128)(2,1)S(1)}, bf16[18,32,128]{2,1,0:T(8,128)(2,1)S(1)}, u32[]{:S(2)}, u32[]{:S(2)}) %collective-permute-start) | collective-permute-done | bytes 147488 | tf_op jit(solution)/shard_map/ppermute | solution.py:199
  7.6 4.0 %copy-done = bf16[1,18,18,128,128]{4,3,2,1,0:T(8,128)(2,1)S(1)} copy-done((bf16[1,18,18,128,128]{4,3,2,1,0:T(8,128)(2,1)S(1)}, bf16[1,18,18,128,128]{4,3,2,1,0:T(8,128)(2,1)}, u32[]{:S(2)}) %copy-start) | copy-done | bytes 10616856
  11.7 0.9 %copy-done.1 = bf16[1,32,2304]{2,1,0:T(8,128)(2,1)S(1)} copy-done((bf16[1,32,2304]{2,1,0:T(8,128)(2,1)S(1)}, bf16[1,32,2304]{2,1,0:T(8,128)(2,1)}, u32[]{:S(2)}) %copy-start.1) | copy-done | bytes 147480
  12.6 0.7 copy-done.3
  13.3 0.7 copy-done.4
  14.0 0.7 copy-done.5
  14.7 2.4 %shard_map.105.refs_0_.own1_ref = f32[9,40,128]{2,1,0:T(8,128)S(1)} custom-call(s32[18,1,18]{2,1,0:T(1,128)S(1)} %bitcast.22, bf16[18,18,128,128]{3,2,1,0:T(8,128)(2,1)S(1)} %bitcast.8, bf16[18,32,128]{2,1,0:T(8,128)(2,1)S(1)} %get-tuple-element.12.own_ref, bf16[18,32,128]{2,1,0:T(8,128)(2,1)S(1)} %collective-permute-done.other_ref, ...), custom_call_target="tpu_custom_call" | custom-call | tf_op jit(solution)/shard_map/pallas_call | solution.py:187
  17.1 2.4 %shard_map.106.own0_ref = f32[9,40,128]{2,1,0:T(8,128)S(1)} custom-call(s32[18,1,18]{2,1,0:T(1,128)S(1)} %bitcast.23, bf16[18,18,128,128]{3,2,1,0:T(8,128)(2,1)S(1)} %bitcast.9, bf16[18,32,128]{2,1,0:T(8,128)(2,1)S(1)} %get-tuple-element.12.own_ref, bf16[18,32,128]{2,1,0:T(8,128)(2,1)S(1)} %collective-permute-done.other_ref, ...), custom_call_target="tpu_custom_call" | custom-call | tf_op jit(solution)/shard_map/pallas_call | solution.py:187
  19.6 1.6 %collective-permute-start.1 = (f32[9,40,128]{2,1,0:T(8,128)S(1)}, f32[9,40,128]{2,1,0:T(8,128)S(1)}, u32[]{:S(2)}, u32[]{:S(2)}) collective-permute-start(f32[9,40,128]{2,1,0:T(8,128)S(1)} %shard_map.106.own0_ref), channel_id=1, source_target_pairs={{0,2},{2,0},{4,6},{6,4},{8,10},{10,8},{12,14},{14,12},{16,18},{18,... | collective-permute-start | bytes 552968 | tf_op jit(solution)/shard_map/ppermute | solution.py:203
  21.2 3.1 %collective-permute-start.2 = (f32[9,40,128]{2,1,0:T(8,128)S(1)}, f32[9,40,128]{2,1,0:T(8,128)S(1)}, u32[]{:S(2)}, u32[]{:S(2)}) collective-permute-start(f32[9,40,128]{2,1,0:T(8,128)S(1)} %shard_map.105.refs_0_.own1_ref), channel_id=1, source_target_pairs={{2,4},{4,2},{6,8},{8,6},{10,12},{12,10},{14,16},{16,14},{18,20},{2... | collective-permute-start | bytes 552968 | tf_op jit(solution)/shard_map/ppermute | solution.py:201
  24.3 5.7 %collective-permute-done.2.mate1_ref = f32[9,40,128]{2,1,0:T(8,128)S(1)} collective-permute-done((f32[9,40,128]{2,1,0:T(8,128)S(1)}, f32[9,40,128]{2,1,0:T(8,128)S(1)}, u32[]{:S(2)}, u32[]{:S(2)}) %collective-permute-start.2) | collective-permute-done | bytes 184352 | tf_op jit(solution)/shard_map/ppermute | solution.py:201
  30.0 1.0 %shard_map.107 = (f32[18,32,128]{2,1,0:T(8,128)S(1)}, bf16[18,32,128]{2,1,0:T(8,128)(2,1)S(1)}, f32[1,2304]{1,0:T(1,128)S(1)}, f32[1,2304]{1,0:T(1,128)S(1)}) custom-call(s32[1,18]{1,0:T(1,128)S(1)} %copy-done.9, s32[1,2304]{1,0:T(1,128)S(1)} %bitcast.30, f32[9,40,128]{2,1,0:T(8,128)S(1)} %shard_map.106.own0_ref, ...), custom_call_target="tpu_custom_call" | custom-call | tf_op jit(solution)/shard_map/pallas_call | solution.py:207
  31.0 0.3 collective-permute-start.3
  31.3 4.8 %collective-permute-done.3.other_ref = bf16[18,32,128]{2,1,0:T(8,128)(2,1)S(1)} collective-permute-done((bf16[18,32,128]{2,1,0:T(8,128)(2,1)S(1)}, bf16[18,32,128]{2,1,0:T(8,128)(2,1)S(1)}, u32[]{:S(2)}, u32[]{:S(2)}) %collective-permute-start.3) | collective-permute-done | bytes 147488 | tf_op jit(solution)/shard_map/ppermute | solution.py:199
  36.2 2.4 %shard_map.108.refs_0_.own1_ref = f32[9,32,128]{2,1,0:T(8,128)S(1)} custom-call(s32[18,1,18]{2,1,0:T(1,128)S(1)} %bitcast.24, bf16[18,18,128,128]{3,2,1,0:T(8,128)(2,1)S(1)} %bitcast.12, bf16[18,32,128]{2,1,0:T(8,128)(2,1)S(1)} %get-tuple-element.14.own_ref, bf16[18,32,128]{2,1,0:T(8,128)(2,1)S(1)} %collective-permute-done.3.other_ref, ...), custom_call_target="tpu_custom_call" | custom-call | tf_op jit(solution)/shard_map/pallas_call | solution.py:187
  38.6 2.4 %shard_map.109.own0_ref = f32[9,32,128]{2,1,0:T(8,128)S(1)} custom-call(s32[18,1,18]{2,1,0:T(1,128)S(1)} %bitcast.25, bf16[18,18,128,128]{3,2,1,0:T(8,128)(2,1)S(1)} %bitcast.13, bf16[18,32,128]{2,1,0:T(8,128)(2,1)S(1)} %get-tuple-element.14.own_ref, bf16[18,32,128]{2,1,0:T(8,128)(2,1)S(1)} %collective-permute-done.3.other_ref, ...), custom_call_target="tpu_custom_call" | custom-call | tf_op jit(solution)/shard_map/pallas_call | solution.py:187
  41.1 0.3 collective-permute-start.4
  41.4 1.9 %collective-permute-start.5 = (f32[9,32,128]{2,1,0:T(8,128)S(1)}, f32[9,32,128]{2,1,0:T(8,128)S(1)}, u32[]{:S(2)}, u32[]{:S(2)}) collective-permute-start(f32[9,32,128]{2,1,0:T(8,128)S(1)} %shard_map.108.refs_0_.own1_ref), channel_id=1, source_target_pairs={{2,4},{4,2},{6,8},{8,6},{10,12},{12,10},{14,16},{16,14},{18,20},{2... | collective-permute-start | bytes 442376 | tf_op jit(solution)/shard_map/ppermute | solution.py:201
  43.4 6.1 %collective-permute-done.5.mate1_ref = f32[9,32,128]{2,1,0:T(8,128)S(1)} collective-permute-done((f32[9,32,128]{2,1,0:T(8,128)S(1)}, f32[9,32,128]{2,1,0:T(8,128)S(1)}, u32[]{:S(2)}, u32[]{:S(2)}) %collective-permute-start.5) | collective-permute-done | bytes 147488 | tf_op jit(solution)/shard_map/ppermute | solution.py:201
  49.5 0.9 %shard_map.110 = (f32[18,32,128]{2,1,0:T(8,128)S(1)}, bf16[18,32,128]{2,1,0:T(8,128)(2,1)S(1)}) custom-call(s32[1,18]{1,0:T(1,128)S(1)} %copy-done.9, s32[1,2304]{1,0:T(1,128)S(1)} %bitcast.31, f32[9,32,128]{2,1,0:T(8,128)S(1)} %shard_map.109.own0_ref, f32[9,32,128]{2,1,0:T(8,128)S(1)} %shard_map.108.refs_0_.own1_ref, ...), custom_call_target="tpu_custom_call" | custom-call | tf_op jit(solution)/shard_map/pallas_call | solution.py:207
  50.4 0.3 collective-permute-start.6
  50.7 5.5 %collective-permute-done.6.other_ref = bf16[18,32,128]{2,1,0:T(8,128)(2,1)S(1)} collective-permute-done((bf16[18,32,128]{2,1,0:T(8,128)(2,1)S(1)}, bf16[18,32,128]{2,1,0:T(8,128)(2,1)S(1)}, u32[]{:S(2)}, u32[]{:S(2)}) %collective-permute-start.6) | collective-permute-done | bytes 147488 | tf_op jit(solution)/shard_map/ppermute | solution.py:199
  56.2 2.4 %shard_map.111.refs_0_.own1_ref = f32[9,32,128]{2,1,0:T(8,128)S(1)} custom-call(s32[18,1,18]{2,1,0:T(1,128)S(1)} %bitcast.26, bf16[18,18,128,128]{3,2,1,0:T(8,128)(2,1)S(1)} %bitcast.14, bf16[18,32,128]{2,1,0:T(8,128)(2,1)S(1)} %get-tuple-element.18.own_ref, bf16[18,32,128]{2,1,0:T(8,128)(2,1)S(1)} %collective-permute-done.6.other_ref, ...), custom_call_target="tpu_custom_call" | custom-call | tf_op jit(solution)/shard_map/pallas_call | solution.py:187
  58.6 2.4 %shard_map.112.own0_ref = f32[9,32,128]{2,1,0:T(8,128)S(1)} custom-call(s32[18,1,18]{2,1,0:T(1,128)S(1)} %bitcast.27, bf16[18,18,128,128]{3,2,1,0:T(8,128)(2,1)S(1)} %bitcast.15, bf16[18,32,128]{2,1,0:T(8,128)(2,1)S(1)} %get-tuple-element.18.own_ref, bf16[18,32,128]{2,1,0:T(8,128)(2,1)S(1)} %collective-permute-done.6.other_ref, ...), custom_call_target="tpu_custom_call" | custom-call | tf_op jit(solution)/shard_map/pallas_call | solution.py:187
  61.1 0.6 collective-permute-start.7
  61.7 1.9 %collective-permute-start.8 = (f32[9,32,128]{2,1,0:T(8,128)S(1)}, f32[9,32,128]{2,1,0:T(8,128)S(1)}, u32[]{:S(2)}, u32[]{:S(2)}) collective-permute-start(f32[9,32,128]{2,1,0:T(8,128)S(1)} %shard_map.111.refs_0_.own1_ref), channel_id=1, source_target_pairs={{2,4},{4,2},{6,8},{8,6},{10,12},{12,10},{14,16},{16,14},{18,20},{2... | collective-permute-start | bytes 442376 | tf_op jit(solution)/shard_map/ppermute | solution.py:201
  63.6 6.1 %collective-permute-done.8.mate1_ref = f32[9,32,128]{2,1,0:T(8,128)S(1)} collective-permute-done((f32[9,32,128]{2,1,0:T(8,128)S(1)}, f32[9,32,128]{2,1,0:T(8,128)S(1)}, u32[]{:S(2)}, u32[]{:S(2)}) %collective-permute-start.8) | collective-permute-done | bytes 147488 | tf_op jit(solution)/shard_map/ppermute | solution.py:201
  69.7 1.7 %shard_map.113 = (bf16[32,2304]{1,0:T(8,128)(2,1)}, bf16[32,2304]{1,0:T(8,128)(2,1)}) custom-call(s32[1,18]{1,0:T(1,128)S(1)} %copy-done.9, s32[1,2304]{1,0:T(1,128)S(1)} %bitcast.32, f32[9,32,128]{2,1,0:T(8,128)S(1)} %shard_map.112.own0_ref, f32[9,32,128]{2,1,0:T(8,128)S(1)} %shard_map.111.refs_0_.own1_ref, ...), custom_call_target="tpu_custom_call" | custom-call | tf_op jit(solution)/shard_map/pallas_call | solution.py:207
  (23 shorter events, 0.1 us)
Async XLA Ops:
  0.6 0.9 %copy-start.6 = (bf16[1,32,2304]{2,1,0:T(8,128)(2,1)S(1)}, bf16[1,32,2304]{2,1,0:T(8,128)(2,1)}, u32[]{:S(2)}) copy-start(bf16[1,32,2304]{2,1,0:T(8,128)(2,1)} %param.12) | copy-start | bytes 442372
  1.5 0.9 %copy-start.7 = (bf16[1,32,2304]{2,1,0:T(8,128)(2,1)S(1)}, bf16[1,32,2304]{2,1,0:T(8,128)(2,1)}, u32[]{:S(2)}) copy-start(bf16[1,32,2304]{2,1,0:T(8,128)(2,1)} %param.13) | copy-start | bytes 442372
  2.9 4.8 %collective-permute-start = (bf16[18,32,128]{2,1,0:T(8,128)(2,1)S(1)}, bf16[18,32,128]{2,1,0:T(8,128)(2,1)S(1)}, u32[]{:S(2)}, u32[]{:S(2)}) collective-permute-start(bf16[18,32,128]{2,1,0:T(8,128)(2,1)S(1)} %get-tuple-element.12.own_ref), channel_id=1, source_target_pairs={{0,1},{1,0},{2,3},{3,2},{4,5},{5,4},{6,7},{7,6},{8,9},{9,8},{10,11... | collective-permute-start | bytes 442376 | tf_op jit(solution)/shard_map/ppermute | solution.py:199
  7.6 4.0 %copy-start = (bf16[1,18,18,128,128]{4,3,2,1,0:T(8,128)(2,1)S(1)}, bf16[1,18,18,128,128]{4,3,2,1,0:T(8,128)(2,1)}, u32[]{:S(2)}) copy-start(bf16[1,18,18,128,128]{4,3,2,1,0:T(8,128)(2,1)} %param.9) | copy-start | bytes 31850500
  11.7 0.9 %copy-start.1 = (bf16[1,32,2304]{2,1,0:T(8,128)(2,1)S(1)}, bf16[1,32,2304]{2,1,0:T(8,128)(2,1)}, u32[]{:S(2)}) copy-start(bf16[1,32,2304]{2,1,0:T(8,128)(2,1)} %param.11) | copy-start | bytes 442372
  12.6 0.7 copy-start.3
  13.3 0.7 copy-start.4
  14.0 0.7 copy-start.5
  14.7 15.3 %copy-start.8 = (s32[1,18,128]{2,0,1:T(1,128)S(1)}, s32[1,18,128]{2,0,1:T(1,128)}, u32[]{:S(2)}) copy-start(s32[1,18,128]{2,0,1:T(1,128)} %param.17) | copy-start | bytes 27652
  14.7 15.3 %copy-start.9 = (s32[1,18]{1,0:T(1,128)S(1)}, s32[1,18]{1,0:T(1,128)}, u32[]{:S(2)}) copy-start(s32[1,18]{1,0:T(1,128)} %partner_ref.5) | copy-start | bytes 220
  14.7 21.5 %slice-start = ((s8[10616832]{0:T(1024)(128)(4,1)}), s8[4194304]{0:T(1024)(128)(4,1)S(1)}, s32[]{:S(2)}) async-start(s8[10616832]{0:T(1024)(128)(4,1)} %bitcast.10), calls=%async_computation | async-start | bytes 8388608
  14.7 21.5 %slice-start.1 = ((s8[10616832]{0:T(1024)(128)(4,1)}), s8[4194304]{0:T(1024)(128)(4,1)S(1)}, s32[]{:S(2)}) async-start(s8[10616832]{0:T(1024)(128)(4,1)} %bitcast.10), calls=%async_computation.1 | async-start | bytes 8388608
  14.7 21.5 %copy-start.2 = (bf16[1,32,2304]{2,1,0:T(8,128)(2,1)S(1)}, bf16[1,32,2304]{2,1,0:T(8,128)(2,1)}, u32[]{:S(2)}) copy-start(bf16[1,32,2304]{2,1,0:T(8,128)(2,1)} %param.11) | copy-start | bytes 442372
  17.1 19.0 %slice-start.2 = ((s8[10616832]{0:T(1024)(128)(4,1)}), s8[2228224]{0:T(1024)(128)(4,1)S(1)}, s32[]{:S(2)}) async-start(s8[10616832]{0:T(1024)(128)(4,1)} %bitcast.10), calls=%async_computation.2 | async-start | bytes 4456448
  19.6 4.7 %collective-permute-start.1 = (f32[9,40,128]{2,1,0:T(8,128)S(1)}, f32[9,40,128]{2,1,0:T(8,128)S(1)}, u32[]{:S(2)}, u32[]{:S(2)}) collective-permute-start(f32[9,40,128]{2,1,0:T(8,128)S(1)} %shard_map.106.own0_ref), channel_id=1, source_target_pairs={{0,2},{2,0},{4,6},{6,4},{8,10},{10,8},{12,14},{14,12},{16,18},{18,... | collective-permute-start | bytes 552968 | tf_op jit(solution)/shard_map/ppermute | solution.py:203
  21.2 8.8 %collective-permute-start.2 = (f32[9,40,128]{2,1,0:T(8,128)S(1)}, f32[9,40,128]{2,1,0:T(8,128)S(1)}, u32[]{:S(2)}, u32[]{:S(2)}) collective-permute-start(f32[9,40,128]{2,1,0:T(8,128)S(1)} %shard_map.105.refs_0_.own1_ref), channel_id=1, source_target_pairs={{2,4},{4,2},{6,8},{8,6},{10,12},{12,10},{14,16},{16,14},{18,20},{2... | collective-permute-start | bytes 552968 | tf_op jit(solution)/shard_map/ppermute | solution.py:201
  31.0 5.2 %collective-permute-start.3 = (bf16[18,32,128]{2,1,0:T(8,128)(2,1)S(1)}, bf16[18,32,128]{2,1,0:T(8,128)(2,1)S(1)}, u32[]{:S(2)}, u32[]{:S(2)}) collective-permute-start(bf16[18,32,128]{2,1,0:T(8,128)(2,1)S(1)} %get-tuple-element.14.own_ref), channel_id=1, source_target_pairs={{0,1},{1,0},{2,3},{3,2},{4,5},{5,4},{6,7},{7,6},{8,9},{9,8},{10,11... | collective-permute-start | bytes 442376 | tf_op jit(solution)/shard_map/ppermute | solution.py:199
  41.1 2.3 %collective-permute-start.4 = (f32[9,32,128]{2,1,0:T(8,128)S(1)}, f32[9,32,128]{2,1,0:T(8,128)S(1)}, u32[]{:S(2)}, u32[]{:S(2)}) collective-permute-start(f32[9,32,128]{2,1,0:T(8,128)S(1)} %shard_map.109.own0_ref), channel_id=1, source_target_pairs={{0,2},{2,0},{4,6},{6,4},{8,10},{10,8},{12,14},{14,12},{16,18},{18,... | collective-permute-start | bytes 442376 | tf_op jit(solution)/shard_map/ppermute | solution.py:203
  41.4 8.0 %collective-permute-start.5 = (f32[9,32,128]{2,1,0:T(8,128)S(1)}, f32[9,32,128]{2,1,0:T(8,128)S(1)}, u32[]{:S(2)}, u32[]{:S(2)}) collective-permute-start(f32[9,32,128]{2,1,0:T(8,128)S(1)} %shard_map.108.refs_0_.own1_ref), channel_id=1, source_target_pairs={{2,4},{4,2},{6,8},{8,6},{10,12},{12,10},{14,16},{16,14},{18,20},{2... | collective-permute-start | bytes 442376 | tf_op jit(solution)/shard_map/ppermute | solution.py:201
  50.4 5.8 %collective-permute-start.6 = (bf16[18,32,128]{2,1,0:T(8,128)(2,1)S(1)}, bf16[18,32,128]{2,1,0:T(8,128)(2,1)S(1)}, u32[]{:S(2)}, u32[]{:S(2)}) collective-permute-start(bf16[18,32,128]{2,1,0:T(8,128)(2,1)S(1)} %get-tuple-element.18.own_ref), channel_id=1, source_target_pairs={{0,1},{1,0},{2,3},{3,2},{4,5},{5,4},{6,7},{7,6},{8,9},{9,8},{10,11... | collective-permute-start | bytes 442376 | tf_op jit(solution)/shard_map/ppermute | solution.py:199
  61.1 2.5 %collective-permute-start.7 = (f32[9,32,128]{2,1,0:T(8,128)S(1)}, f32[9,32,128]{2,1,0:T(8,128)S(1)}, u32[]{:S(2)}, u32[]{:S(2)}) collective-permute-start(f32[9,32,128]{2,1,0:T(8,128)S(1)} %shard_map.112.own0_ref), channel_id=1, source_target_pairs={{0,2},{2,0},{4,6},{6,4},{8,10},{10,8},{12,14},{14,12},{16,18},{18,... | collective-permute-start | bytes 442376 | tf_op jit(solution)/shard_map/ppermute | solution.py:203
  61.7 8.0 %collective-permute-start.8 = (f32[9,32,128]{2,1,0:T(8,128)S(1)}, f32[9,32,128]{2,1,0:T(8,128)S(1)}, u32[]{:S(2)}, u32[]{:S(2)}) collective-permute-start(f32[9,32,128]{2,1,0:T(8,128)S(1)} %shard_map.111.refs_0_.own1_ref), channel_id=1, source_target_pairs={{2,4},{4,2},{6,8},{8,6},{10,12},{12,10},{14,16},{16,14},{18,20},{2... | collective-permute-start | bytes 442376 | tf_op jit(solution)/shard_map/ppermute | solution.py:201

commit v3 on v2

v3 whole, which is shorter than its diff:
```python
import functools

import jax
import jax.numpy as jnp
from jax import lax
from jax.experimental import pallas as pl
from jax.experimental.pallas import tpu as pltpu
from jax.sharding import PartitionSpec as P

ITERS = 3
SUBLANES = 8
VMEM_BYTES = 24 * 2**20

ONSET_JUMP = 0.15
FAILURE_JUMP = 1.5

VMEM = pl.BlockSpec(memory_space=pltpu.VMEM)
SMEM = pl.BlockSpec(memory_space=pltpu.SMEM)
ANY = pl.BlockSpec(memory_space=pl.ANY)


def position(group):
    near = group * (lax.axis_index("sub") % 2)
    return near, group - near, lax.axis_index("row")


def lanes_of(face, extent):
    return pl.ds(pl.multiple_of(face * extent, extent), extent)


def prepare(motion_hbm, stress_hbm, load_hbm, stiff_hbm, record_hbm, turn_hbm, columns_hbm, partner_hbm,
            robin0_ref, robin1_ref, half0_ref, half1_ref, load_ref, stiff_ref, record_ref, turn_ref, columns_ref, partner_ref,
            motion_ref, stress_ref, sems):
    pairs = (
        (motion_hbm, motion_ref), (stress_hbm, stress_ref), (load_hbm, load_ref), (stiff_hbm, stiff_ref),
        (record_hbm, record_ref), (turn_hbm, turn_ref), (columns_hbm, columns_ref), (partner_hbm, partner_ref),
    )
    copies = [pltpu.make_async_copy(source, target, sems.at[n]) for n, (source, target) in enumerate(pairs)]
    for copy in copies:
        copy.start()
    for copy in copies[:2]:
        copy.wait()
    group, _, extent = robin0_ref.shape
    starts = position(group)
    for side, (robin_ref, half_ref) in enumerate(((robin0_ref, half0_ref), (robin1_ref, half1_ref))):
        for index in range(group):
            lanes = lanes_of(starts[side] + index, extent)
            robin = stress_ref[:, lanes].astype(jnp.float32) + motion_ref[:, lanes].astype(jnp.float32)
            robin_ref[index] = robin
            half_ref[index] = robin.astype(jnp.bfloat16)
    for copy in copies[2:]:
        copy.wait()


def fetch(blocks_hbm, blocks_ref, sems):
    copies = [
        pltpu.make_async_copy(blocks_hbm.at[face], blocks_ref.at[face], sems.at[face])
        for face in range(blocks_hbm.shape[0])
    ]
    for copy in copies:
        copy.start()
    for copy in copies:
        copy.wait()


def block_products(parts):
    times, extent = parts[0][0][0].shape
    zero = jnp.zeros_like(parts[0][0][1])
    depth = max(len(part) for part in parts)
    parts = [part + [(part[0][0], zero)] * (depth - len(part)) for part in parts]
    values = jnp.concatenate([jnp.concatenate([v for v, _ in part], axis=1) for part in parts], axis=0)
    blocks = jnp.concatenate([jnp.concatenate([c for _, c in part], axis=1) for part in parts], axis=0)
    product = lax.dot_general(values, blocks, (((1,), (1,)), ((), ())), preferred_element_type=jnp.float32)
    return [
        product[p * times : (p + 1) * times, p * extent : (p + 1) * extent] for p in range(len(parts))
    ]


def linear_section(side, columns_ref, compliance_ref, own0_ref, own1_ref, other0_ref, other1_ref, robin_ref, load_ref,
                   stiff_ref, record_ref, *refs):
    out_ref, half_ref = refs[-2:]
    group, rows, extent = out_ref.shape
    times = own0_ref.shape[1]
    faces, stored = compliance_ref.shape[:2]
    *starts, mine = position(group)
    first = starts[side]
    for run, refs in ((mine, (own0_ref, own1_ref)), (1 - mine, (other0_ref, other1_ref))):
        for start, ref in zip(starts, refs):
            half_ref[pl.ds(run * faces + start, group)] = ref[...]

    def entries(face, begin, end):
        return [(half_ref[columns_ref[face, 0, j]], compliance_ref[face, j]) for j in range(begin, end)]

    def finish(index, product):
        lanes = lanes_of(first + index, extent)
        response = product + load_ref[:, lanes].astype(jnp.float32)
        out_ref[index, :times] = robin_ref[index] - 2.0 * response
        if rows > times:
            out_ref[index, times : times + 1] = stiff_ref[:, lanes]
            out_ref[index, times + 1 : times + 2] = record_ref[:, lanes]
            out_ref[index, times + 2 :] = jnp.zeros_like(out_ref[index, times + 2 :])

    for index in range(0, group - 1, 2):
        pair = block_products([entries(first + index + k, 0, stored) for k in range(2)])
        for k in range(2):
            finish(index + k, pair[k])
    if group % 2:
        face = first + group - 1
        cut = (stored + 3) // 4 * 2
        finish(group - 1, sum(block_products([entries(face, 0, cut), entries(face, cut, stored)])))


def running_peak(sizes):
    row = lax.broadcasted_iota(jnp.int32, sizes.shape, 0)
    step = 1
    while step < sizes.shape[0]:
        earlier = pltpu.roll(sizes, step, 0)
        sizes = jnp.maximum(sizes, jnp.where(row >= step, earlier, 0.0))
        step *= 2
    return sizes


def local_face(times, ascent, mate, turn, stiffness, record, live, begin):
    extent = ascent.shape[1]
    gather = functools.partial(jnp.take_along_axis, axis=1, mode="promise_in_bounds")
    mate_ascent = gather(mate[:times], jnp.broadcast_to(turn, (times, extent)))
    if begin:
        constants = gather(mate[times:], jnp.broadcast_to(turn, (SUBLANES, extent)))
        stiffness = 0.5 * (stiffness + constants[:1])
        record = jnp.maximum(record, constants[1:2])
    difference = ascent - mate_ascent
    jump = difference / (1.0 + 2.0 * stiffness)
    peak = jnp.maximum(record, running_peak(jnp.abs(jump)))
    damage = jnp.clip((peak - ONSET_JUMP) / (FAILURE_JUMP - ONSET_JUMP), 0.0, 1.0)
    effective = stiffness * (1.0 - damage)
    traction = jnp.where(live, effective * difference / (1.0 + 2.0 * effective), 0.0)
    return traction, traction - ascent, stiffness, record


def local_group(side, begin, partner_ref, turn_ref, own_ref, mate_ref, stiff_ref, record_ref, robin_ref, half_ref, *pair_refs):
    group, times, extent = robin_ref.shape
    first = position(group)[side]
    for index in range(group):
        face = first + index
        partner = partner_ref[0, face]
        constants = lanes_of(face if begin else index, extent)
        traction, motion, stiffness, record = local_face(
            times, own_ref[index, :times], mate_ref[jnp.maximum(partner, 0)], turn_ref[:, lanes_of(face, extent)],
            stiff_ref[:, constants], record_ref[:, constants], partner >= 0, begin,
        )
        robin = traction + motion
        robin_ref[index] = robin
        half_ref[index] = robin.astype(jnp.bfloat16)
        if begin:
            pair_refs[0][:, lanes_of(index, extent)] = stiffness
            pair_refs[1][:, lanes_of(index, extent)] = record


def local_last(partner_ref, turn_ref, own0_ref, own1_ref, mate0_ref, mate1_ref, stiff0_ref, stiff1_ref,
               record0_ref, record1_ref, motion_ref, traction_ref):
    group, times, extent = own0_ref.shape
    starts = position(group)
    for side, (own_ref, mate_ref, stiff_ref, record_ref) in enumerate((
        (own0_ref, mate0_ref, stiff0_ref, record0_ref), (own1_ref, mate1_ref, stiff1_ref, record1_ref),
    )):
        for index in range(group):
            face = starts[side] + index
            lanes, constants = lanes_of(face, extent), lanes_of(index, extent)
            partner = partner_ref[0, face]
            traction, motion, _, _ = local_face(
                times, own_ref[index], mate_ref[jnp.maximum(partner, 0)], turn_ref[:, lanes],
                stiff_ref[:, constants], record_ref[:, constants], partner >= 0, False,
            )
            motion_ref[:, lanes] = motion.astype(jnp.bfloat16)
            traction_ref[:, lanes] = traction.astype(jnp.bfloat16)


def shards(
    compliance,
    block_columns,
    load_response,
    starting_motion,
    start_traction,
    stiffness,
    history,
    face_partner,
    orientation,
):
    _, faces, stored, extent, _ = compliance.shape
    times = starting_motion.shape[1]
    group = faces // 2
    subs = lax.axis_size("sub")
    rows = lax.axis_size("row")
    near_pairs = [(s, s ^ 1 if s ^ 1 < subs else s) for s in range(subs)]
    far_mate = [s - 1 if s % 2 == 0 else s + 1 for s in range(subs)]
    far_pairs = [(s, t if 0 <= t < subs else s) for s, t in enumerate(far_mate)]
    swap = [(r, rows - 1 - r) for r in range(rows)]

    def f32(*shape):
        return jax.ShapeDtypeStruct(shape, jnp.float32)

    def bf16(*shape):
        return jax.ShapeDtypeStruct(shape, jnp.bfloat16)

    def s32(*shape):
        return jax.ShapeDtypeStruct(shape, jnp.int32)

    def call(kernel, in_specs, out_shape, scratch=(), moved=0):
        outs = out_shape if isinstance(out_shape, tuple) else (out_shape,)
        return pl.pallas_call(
            kernel,
            out_shape=out_shape,
            in_specs=in_specs,
            out_specs=(VMEM,) * len(outs) if isinstance(out_shape, tuple) else VMEM,
            scratch_shapes=scratch,
            compiler_params=pltpu.CompilerParams(vmem_limit_bytes=VMEM_BYTES),
            cost_estimate=pl.CostEstimate(flops=0, bytes_accessed=moved, transcendentals=0),
        )

    part = (group, times, extent)
    flat = (times, faces * extent)
    block_bytes = faces * stored * extent * extent * 2
    part_bytes = group * times * extent * 4
    robin0, robin1, half0, half1, load, stiff, record, turn, columns, partner = call(
        prepare, [ANY] * 8,
        (f32(*part), f32(*part), bf16(*part), bf16(*part), bf16(*flat), f32(1, faces * extent), f32(1, faces * extent),
         s32(1, faces * extent), s32(faces, 1, stored), s32(1, faces)),
        [pltpu.VMEM(flat, jnp.bfloat16), pltpu.VMEM(flat, jnp.bfloat16), pltpu.SemaphoreType.DMA((8,))],
        8 * part_bytes,
    )(
        starting_motion[0], start_traction[0], load_response[0], stiffness, history,
        orientation.reshape(1, -1), jnp.transpose(block_columns, (1, 0, 2)), face_partner,
    )
    blocks = call(
        fetch, [ANY], pltpu.VMEM((faces, stored, extent, extent), jnp.bfloat16),
        [pltpu.SemaphoreType.DMA((faces,))], block_bytes,
    )(compliance[0])

    robin, half = [robin0, robin1], [half0, half1]
    stiffs, records = [stiff, stiff], [record, record]
    for iteration in range(ITERS):
        begin, last = iteration == 0, iteration == ITERS - 1
        other = [lax.ppermute(half[side], "row", swap) for side in range(2)]
        ascent, mates = [None, None], [None, None]
        for side, pairs in ((1, far_pairs), (0, near_pairs)):
            after = () if side else (ascent[1],)
            ascent[side] = call(
                functools.partial(linear_section, side),
                [SMEM] + [VMEM] * 9 + [ANY] * len(after),
                f32(group, times + SUBLANES if begin else times, extent),
                [pltpu.VMEM((rows * faces, times, extent), jnp.bfloat16)],
                2 * block_bytes,
            )(columns, blocks, *half, *other, robin[side], load, stiff, record, *after)
            mates[side] = lax.ppermute(ascent[side], "sub", pairs)
        if last:
            return tuple(out[None] for out in call(
                local_last, [SMEM] + [VMEM] * 9, (bf16(*flat),) * 2, (), 8 * part_bytes,
            )(partner, turn, *ascent, *mates, *stiffs, *records))
        for side in range(2):
            outs = (f32(*part), bf16(*part))
            if begin:
                outs += (f32(1, group * extent),) * 2
            robin[side], half[side], *pair = call(
                functools.partial(local_group, side, begin), [SMEM] + [VMEM] * 5, outs, (), 8 * part_bytes,
            )(partner, turn, ascent[side], mates[side], stiffs[side], records[side])
            if begin:
                stiffs[side], records[side] = pair


def solution(mesh):
    in_specs = (
        P("sub", "row", None, None, None),
        P("sub", "row", None),
        P("sub", None, "row"),
        P("sub", None, "row"),
        P("sub", None, "row"),
        P("sub", "row"),
        P("sub", "row"),
        P("sub", "row"),
        P("sub", "row", None),
    )
    out_specs = (P("sub", None, "row"), P("sub", None, "row"))
    return jax.shard_map(shards, mesh=mesh, in_specs=in_specs, out_specs=out_specs, check_vma=False)
```

time: 71.8 us -> 68.8 us (0.958)
  the two profiles are of different devices: /device:TPU:27 before, /device:TPU:25 now
where the time goes in v3:
time: 68.8 us; the launch traced here: 68.4 us
  Pallas kernels  22.6 us (33%)
  waiting for transfers between devices  18.7 us (27%)
  starting transfers between devices  16 us (23%)
  local copies, waits for them, and re-layouts  10.2 us (15%)
  between operations  0.82 us (1%)
    pallas_call x6, Pallas kernels, shards(): call(functools.partial(linear_section, side), [SMEM] + [VMEM] * 9 + [ANY]...  14.6 us
    ppermute x6, waiting for transfers between devices, shards(): mates[side] = lax.ppermute(ascent[side], 'sub', pairs)  13.7 us
    unnamed x18, local copies, waits for them, and re-layouts  10.2 us
    ppermute x6, starting transfers between devices, shards(): mates[side] = lax.ppermute(ascent[side], 'sub', pairs)  9.39 us
    ppermute x6, starting transfers between devices, shards(): other = [lax.ppermute(half[side], 'row', swap) for side in range(2)]  6.65 us
    ppermute x6, waiting for transfers between devices, shards(): other = [lax.ppermute(half[side], 'row', swap) for side in range(2)]  5.01 us
    pallas_call x4, Pallas kernels, shards(): call(functools.partial(local_group, side, begin), [SMEM] + [VMEM] * 5, ou...  3.23 us
    pallas_call x1, Pallas kernels, shards(): call(fetch, [ANY], pltpu.VMEM((faces, stored, extent, extent), jnp.bfloat...  2.34 us
  transfers between devices with their start and end apart: 12, of which 5 were waited for; matrix products, arithmetic and copies ran while one was open for 0% of the time, Pallas kernels for 8%

profile of v3, /device:TPU:25, one launch (start us, length us, event | category | flops | bytes accessed | tf_op | source)
XLA Modules:
  0.0 68.4 jit_solution(14543487196884691378)
XLA Ops:
  0.6 0.9 %copy-done.1 = bf16[1,32,2304]{2,1,0:T(8,128)(2,1)S(1)} copy-done((bf16[1,32,2304]{2,1,0:T(8,128)(2,1)S(1)}, bf16[1,32,2304]{2,1,0:T(8,128)(2,1)}, u32[]{:S(2)}) %copy-start.1) | copy-done | bytes 147480
  1.5 0.9 %copy-done.2 = bf16[1,32,2304]{2,1,0:T(8,128)(2,1)S(1)} copy-done((bf16[1,32,2304]{2,1,0:T(8,128)(2,1)S(1)}, bf16[1,32,2304]{2,1,0:T(8,128)(2,1)}, u32[]{:S(2)}) %copy-start.2) | copy-done | bytes 147480
  2.5 0.9 %copy-done.3 = bf16[1,32,2304]{2,1,0:T(8,128)(2,1)S(1)} copy-done((bf16[1,32,2304]{2,1,0:T(8,128)(2,1)S(1)}, bf16[1,32,2304]{2,1,0:T(8,128)(2,1)}, u32[]{:S(2)}) %copy-start.3) | copy-done | bytes 147480
  3.4 0.7 %copy-done.4 = f32[1,2304]{1,0:T(1,128)S(1)} copy-done((f32[1,2304]{1,0:T(1,128)S(1)}, f32[1,2304]{1,0:T(1,128)}, u32[]{:S(2)}) %copy-start.4) | copy-done | bytes 9240
  6.8 0.8 %shard_map.104 = (f32[9,32,128]{2,1,0:T(8,128)S(1)}, f32[9,32,128]{2,1,0:T(8,128)S(1)}, bf16[9,32,128]{2,1,0:T(8,128)(2,1)S(1)}, bf16[9,32,128]{2,1,0:T(8,128)(2...) custom-call(bf16[32,2304]{1,0:T(8,128)(2,1)S(1)} %bitcast.9, ...), custom_call_target="tpu_custom_call" | custom-call | bytes 1179648 | tf_op jit(solution)/shard_map/pallas_call | solution.py:224
  7.6 1.3 %collective-permute-start = (bf16[9,32,128]{2,1,0:T(8,128)(2,1)S(1)}, bf16[9,32,128]{2,1,0:T(8,128)(2,1)S(1)}, u32[]{:S(2)}, u32[]{:S(2)}) collective-permute-start(bf16[9,32,128]{2,1,0:T(8,128)(2,1)S(1)} %get-tuple-element.29.own0_ref), channel_id=1, source_target_pairs={{0,1},{1,0},{2,3},{3,2},{4,5},{5,4},{6,7},{7,6},{8,9},{9,8},{10,11... | collective-permute-start | bytes 221192 | tf_op jit(solution)/shard_map/ppermute | solution.py:243
  9.1 4.0 %copy-done = bf16[1,18,18,128,128]{4,3,2,1,0:T(8,128)(2,1)S(1)} copy-done((bf16[1,18,18,128,128]{4,3,2,1,0:T(8,128)(2,1)S(1)}, bf16[1,18,18,128,128]{4,3,2,1,0:T(8,128)(2,1)}, u32[]{:S(2)}) %copy-start) | copy-done | bytes 10616856
  13.2 2.3 %shard_map.105.compliance_ref = bf16[18,18,128,128]{3,2,1,0:T(8,128)(2,1)S(1)} custom-call(bf16[18,18,128,128]{3,2,1,0:T(8,128)(2,1)S(1)} %bitcast.8), custom_call_target="tpu_custom_call" | custom-call | bytes 10616832 | tf_op jit(solution)/shard_map/pallas_call | solution.py:234
  15.5 2.4 %shard_map.106.refs_0_.own_ref = f32[9,40,128]{2,1,0:T(8,128)S(1)} custom-call(s32[18,1,18]{2,1,0:T(1,128)S(1)} %get-tuple-element.28.columns_ref, bf16[18,18,128,128]{3,2,1,0:T(8,128)(2,1)S(1)} %shard_map.105.compliance_ref, bf16[9,32,128]{2,1,0:T(8,128)(2,1)S(1)} %get-tuple-element.29.own0_ref, bf16[9,32,128]{2,1,0:T(8,128)(2,1)S(1)} %get-tuple-element.30.own1_ref, ...), custom_call_target="tpu_custom_call" | custom-call | bytes 21233664 | tf_op jit(solution)/shard_map/pallas_call | solution.py:247
  18.0 2.4 %shard_map.107.own_ref = f32[9,40,128]{2,1,0:T(8,128)S(1)} custom-call(s32[18,1,18]{2,1,0:T(1,128)S(1)} %get-tuple-element.28.columns_ref, bf16[18,18,128,128]{3,2,1,0:T(8,128)(2,1)S(1)} %shard_map.105.compliance_ref, bf16[9,32,128]{2,1,0:T(8,128)(2,1)S(1)} %get-tuple-element.29.own0_ref, bf16[9,32,128]{2,1,0:T(8,128)(2,1)S(1)} %get-tuple-element.30.own1_ref, ...), custom_call_target="tpu_custom_call" | custom-call | bytes 21233664 | tf_op jit(solution)/shard_map/pallas_call | solution.py:247
  20.4 1.3 %collective-permute-start.2 = (f32[9,40,128]{2,1,0:T(8,128)S(1)}, f32[9,40,128]{2,1,0:T(8,128)S(1)}, u32[]{:S(2)}, u32[]{:S(2)}) collective-permute-start(f32[9,40,128]{2,1,0:T(8,128)S(1)} %shard_map.107.own_ref), channel_id=1, source_target_pairs={{0,2},{2,0},{4,6},{6,4},{8,10},{10,8},{12,14},{14,12},{16,18},{18,... | collective-permute-start | bytes 552968 | tf_op jit(solution)/shard_map/ppermute | solution.py:254
  21.7 3.0 %collective-permute-start.3 = (f32[9,40,128]{2,1,0:T(8,128)S(1)}, f32[9,40,128]{2,1,0:T(8,128)S(1)}, u32[]{:S(2)}, u32[]{:S(2)}) collective-permute-start(f32[9,40,128]{2,1,0:T(8,128)S(1)} %shard_map.106.refs_0_.own_ref), channel_id=1, source_target_pairs={{0,0},{2,4},{4,2},{6,8},{8,6},{10,12},{12,10},{14,16},{16,14},{18,... | collective-permute-start | bytes 552968 | tf_op jit(solution)/shard_map/ppermute | solution.py:254
  24.8 0.8 %shard_map.108 = (f32[9,32,128]{2,1,0:T(8,128)S(1)}, bf16[9,32,128]{2,1,0:T(8,128)(2,1)S(1)}, f32[1,1152]{1,0:T(1,128)S(1)}, f32[1,1152]{1,0:T(1,128)S(1)}) custom-call(s32[1,18]{1,0:T(1,128)S(1)} %get-tuple-element.26.partner_ref, s32[1,2304]{1,0:T(1,128)S(1)} %get-tuple-element.27.turn_ref, f32[9,40,128]{2,1,0:T(8,128)S(1)} %shard_map.107.own_ref, ...), custom_call_target="tpu_custom_call" | custom-call | bytes 1179648 | tf_op jit(solution)/shard_map/pallas_call | solution.py:263
  25.6 1.3 %collective-permute-start.4 = (bf16[9,32,128]{2,1,0:T(8,128)(2,1)S(1)}, bf16[9,32,128]{2,1,0:T(8,128)(2,1)S(1)}, u32[]{:S(2)}, u32[]{:S(2)}) collective-permute-start(bf16[9,32,128]{2,1,0:T(8,128)(2,1)S(1)} %get-tuple-element.36.own0_ref), channel_id=1, source_target_pairs={{0,1},{1,0},{2,3},{3,2},{4,5},{5,4},{6,7},{7,6},{8,9},{9,8},{10,11... | collective-permute-start | bytes 221192 | tf_op jit(solution)/shard_map/ppermute | solution.py:243
  26.9 3.7 %collective-permute-done.3.mate_ref = f32[9,40,128]{2,1,0:T(8,128)S(1)} collective-permute-done((f32[9,40,128]{2,1,0:T(8,128)S(1)}, f32[9,40,128]{2,1,0:T(8,128)S(1)}, u32[]{:S(2)}, u32[]{:S(2)}) %collective-permute-start.3) | collective-permute-done | bytes 184352 | tf_op jit(solution)/shard_map/ppermute | solution.py:254
  30.5 0.8 %shard_map.109 = (f32[9,32,128]{2,1,0:T(8,128)S(1)}, bf16[9,32,128]{2,1,0:T(8,128)(2,1)S(1)}, f32[1,1152]{1,0:T(1,128)S(1)}, f32[1,1152]{1,0:T(1,128)S(1)}) custom-call(s32[1,18]{1,0:T(1,128)S(1)} %get-tuple-element.26.partner_ref, s32[1,2304]{1,0:T(1,128)S(1)} %get-tuple-element.27.turn_ref, f32[9,40,128]{2,1,0:T(8,128)S(1)} %shard_map.106.refs_0_.own_ref, ...), custom_call_target="tpu_custom_call" | custom-call | bytes 1179648 | tf_op jit(solution)/shard_map/pallas_call | solution.py:263
  31.4 1.3 %collective-permute-start.5 = (bf16[9,32,128]{2,1,0:T(8,128)(2,1)S(1)}, bf16[9,32,128]{2,1,0:T(8,128)(2,1)S(1)}, u32[]{:S(2)}, u32[]{:S(2)}) collective-permute-start(bf16[9,32,128]{2,1,0:T(8,128)(2,1)S(1)} %get-tuple-element.37.own1_ref), channel_id=1, source_target_pairs={{0,1},{1,0},{2,3},{3,2},{4,5},{5,4},{6,7},{7,6},{8,9},{9,8},{10,11... | collective-permute-start | bytes 221192 | tf_op jit(solution)/shard_map/ppermute | solution.py:243
  32.6 2.3 %collective-permute-done.5.other1_ref = bf16[9,32,128]{2,1,0:T(8,128)(2,1)S(1)} collective-permute-done((bf16[9,32,128]{2,1,0:T(8,128)(2,1)S(1)}, bf16[9,32,128]{2,1,0:T(8,128)(2,1)S(1)}, u32[]{:S(2)}, u32[]{:S(2)}) %collective-permute-start.5) | collective-permute-done | bytes 73760 | tf_op jit(solution)/shard_map/ppermute | solution.py:243
  34.9 2.4 %shard_map.110.refs_0_.own_ref = f32[9,32,128]{2,1,0:T(8,128)S(1)} custom-call(s32[18,1,18]{2,1,0:T(1,128)S(1)} %get-tuple-element.28.columns_ref, bf16[18,18,128,128]{3,2,1,0:T(8,128)(2,1)S(1)} %shard_map.105.compliance_ref, bf16[9,32,128]{2,1,0:T(8,128)(2,1)S(1)} %get-tuple-element.36.own0_ref, bf16[9,32,128]{2,1,0:T(8,128)(2,1)S(1)} %get-tuple-element.37.own1_ref, ...), custom_call_target="tpu_custom_call" | custom-call | bytes 21233664 | tf_op jit(solution)/shard_map/pallas_call | solution.py:247
  37.4 2.4 %shard_map.111.own_ref = f32[9,32,128]{2,1,0:T(8,128)S(1)} custom-call(s32[18,1,18]{2,1,0:T(1,128)S(1)} %get-tuple-element.28.columns_ref, bf16[18,18,128,128]{3,2,1,0:T(8,128)(2,1)S(1)} %shard_map.105.compliance_ref, bf16[9,32,128]{2,1,0:T(8,128)(2,1)S(1)} %get-tuple-element.36.own0_ref, bf16[9,32,128]{2,1,0:T(8,128)(2,1)S(1)} %get-tuple-element.37.own1_ref, ...), custom_call_target="tpu_custom_call" | custom-call | bytes 21233664 | tf_op jit(solution)/shard_map/pallas_call | solution.py:247
  40.2 2.3 %collective-permute-start.7 = (f32[9,32,128]{2,1,0:T(8,128)S(1)}, f32[9,32,128]{2,1,0:T(8,128)S(1)}, u32[]{:S(2)}, u32[]{:S(2)}) collective-permute-start(f32[9,32,128]{2,1,0:T(8,128)S(1)} %shard_map.110.refs_0_.own_ref), channel_id=1, source_target_pairs={{0,0},{2,4},{4,2},{6,8},{8,6},{10,12},{12,10},{14,16},{16,14},{18,... | collective-permute-start | bytes 442376 | tf_op jit(solution)/shard_map/ppermute | solution.py:254
  42.5 0.8 %shard_map.112 = (f32[9,32,128]{2,1,0:T(8,128)S(1)}, bf16[9,32,128]{2,1,0:T(8,128)(2,1)S(1)}) custom-call(s32[1,18]{1,0:T(1,128)S(1)} %get-tuple-element.26.partner_ref, s32[1,2304]{1,0:T(1,128)S(1)} %get-tuple-element.27.turn_ref, f32[9,32,128]{2,1,0:T(8,128)S(1)} %shard_map.111.own_ref, f32[9,32,128]{2,1,0:T(8,128)S(1)} %collective-permute-done.6.mate_ref, ...), custom_call_target="tpu_custom_call" | custom-call | bytes 1179648 | tf_op jit(solution)/shard_map/pallas_call | solution.py:263
  43.3 1.3 %collective-permute-start.8 = (bf16[9,32,128]{2,1,0:T(8,128)(2,1)S(1)}, bf16[9,32,128]{2,1,0:T(8,128)(2,1)S(1)}, u32[]{:S(2)}, u32[]{:S(2)}) collective-permute-start(bf16[9,32,128]{2,1,0:T(8,128)(2,1)S(1)} %get-tuple-element.42.own0_ref), channel_id=1, source_target_pairs={{0,1},{1,0},{2,3},{3,2},{4,5},{5,4},{6,7},{7,6},{8,9},{9,8},{10,11... | collective-permute-start | bytes 221192 | tf_op jit(solution)/shard_map/ppermute | solution.py:243
  44.6 3.9 %collective-permute-done.7.mate_ref = f32[9,32,128]{2,1,0:T(8,128)S(1)} collective-permute-done((f32[9,32,128]{2,1,0:T(8,128)S(1)}, f32[9,32,128]{2,1,0:T(8,128)S(1)}, u32[]{:S(2)}, u32[]{:S(2)}) %collective-permute-start.7) | collective-permute-done | bytes 147488 | tf_op jit(solution)/shard_map/ppermute | solution.py:254
  48.5 0.8 %shard_map.113 = (f32[9,32,128]{2,1,0:T(8,128)S(1)}, bf16[9,32,128]{2,1,0:T(8,128)(2,1)S(1)}) custom-call(s32[1,18]{1,0:T(1,128)S(1)} %get-tuple-element.26.partner_ref, s32[1,2304]{1,0:T(1,128)S(1)} %get-tuple-element.27.turn_ref, f32[9,32,128]{2,1,0:T(8,128)S(1)} %shard_map.110.refs_0_.own_ref, f32[9,32,128]{2,1,0:T(8,128)S(1)} %collective-permute-done.7.mate_ref, ...), custom_call_target="tpu_custom_call" | custom-call | bytes 1179648 | tf_op jit(solution)/shard_map/pallas_call | solution.py:263
  49.3 1.3 %collective-permute-start.9 = (bf16[9,32,128]{2,1,0:T(8,128)(2,1)S(1)}, bf16[9,32,128]{2,1,0:T(8,128)(2,1)S(1)}, u32[]{:S(2)}, u32[]{:S(2)}) collective-permute-start(bf16[9,32,128]{2,1,0:T(8,128)(2,1)S(1)} %get-tuple-element.45.own1_ref), channel_id=1, source_target_pairs={{0,1},{1,0},{2,3},{3,2},{4,5},{5,4},{6,7},{7,6},{8,9},{9,8},{10,11... | collective-permute-start | bytes 221192 | tf_op jit(solution)/shard_map/ppermute | solution.py:243
  50.6 2.7 %collective-permute-done.9.other1_ref = bf16[9,32,128]{2,1,0:T(8,128)(2,1)S(1)} collective-permute-done((bf16[9,32,128]{2,1,0:T(8,128)(2,1)S(1)}, bf16[9,32,128]{2,1,0:T(8,128)(2,1)S(1)}, u32[]{:S(2)}, u32[]{:S(2)}) %collective-permute-start.9) | collective-permute-done | bytes 73760 | tf_op jit(solution)/shard_map/ppermute | solution.py:243
  53.3 2.4 %shard_map.114.refs_0_.own1_ref = f32[9,32,128]{2,1,0:T(8,128)S(1)} custom-call(s32[18,1,18]{2,1,0:T(1,128)S(1)} %get-tuple-element.28.columns_ref, bf16[18,18,128,128]{3,2,1,0:T(8,128)(2,1)S(1)} %shard_map.105.compliance_ref, bf16[9,32,128]{2,1,0:T(8,128)(2,1)S(1)} %get-tuple-element.42.own0_ref, bf16[9,32,128]{2,1,0:T(8,128)(2,1)S(1)} %get-tuple-element.45.own1_ref, ...), custom_call_target="tpu_custom_call" | custom-call | bytes 21233664 | tf_op jit(solution)/shard_map/pallas_call | solution.py:247
  55.7 2.4 %shard_map.115.own0_ref = f32[9,32,128]{2,1,0:T(8,128)S(1)} custom-call(s32[18,1,18]{2,1,0:T(1,128)S(1)} %get-tuple-element.28.columns_ref, bf16[18,18,128,128]{3,2,1,0:T(8,128)(2,1)S(1)} %shard_map.105.compliance_ref, bf16[9,32,128]{2,1,0:T(8,128)(2,1)S(1)} %get-tuple-element.42.own0_ref, bf16[9,32,128]{2,1,0:T(8,128)(2,1)S(1)} %get-tuple-element.45.own1_ref, ...), custom_call_target="tpu_custom_call" | custom-call | bytes 21233664 | tf_op jit(solution)/shard_map/pallas_call | solution.py:247
  58.7 1.9 %collective-permute-start.11 = (f32[9,32,128]{2,1,0:T(8,128)S(1)}, f32[9,32,128]{2,1,0:T(8,128)S(1)}, u32[]{:S(2)}, u32[]{:S(2)}) collective-permute-start(f32[9,32,128]{2,1,0:T(8,128)S(1)} %shard_map.114.refs_0_.own1_ref), channel_id=1, source_target_pairs={{0,0},{2,4},{4,2},{6,8},{8,6},{10,12},{12,10},{14,16},{16,14},{18,... | collective-permute-start | bytes 442376 | tf_op jit(solution)/shard_map/ppermute | solution.py:254
  60.6 6.1 %collective-permute-done.11.mate1_ref = f32[9,32,128]{2,1,0:T(8,128)S(1)} collective-permute-done((f32[9,32,128]{2,1,0:T(8,128)S(1)}, f32[9,32,128]{2,1,0:T(8,128)S(1)}, u32[]{:S(2)}, u32[]{:S(2)}) %collective-permute-start.11) | collective-permute-done | bytes 147488 | tf_op jit(solution)/shard_map/ppermute | solution.py:254
  66.7 1.7 %shard_map.116 = (bf16[32,2304]{1,0:T(8,128)(2,1)}, bf16[32,2304]{1,0:T(8,128)(2,1)}) custom-call(s32[1,18]{1,0:T(1,128)S(1)} %get-tuple-element.26.partner_ref, s32[1,2304]{1,0:T(1,128)S(1)} %get-tuple-element.27.turn_ref, f32[9,32,128]{2,1,0:T(8,128)S(1)} %shard_map.115.own0_ref, f32[9,32,128]{2,1,0:T(8,128)S(1)} %shard_map.114.refs_0_.own1_ref, ...), custom_call_target="tpu_custom_call" | custom-call | bytes 1179648 | tf_op jit(solution)/shard_map/pallas_call | solution.py:256
  (23 shorter events, 3.9 us)
Async XLA Ops:
  0.6 0.9 %copy-start.1 = (bf16[1,32,2304]{2,1,0:T(8,128)(2,1)S(1)}, bf16[1,32,2304]{2,1,0:T(8,128)(2,1)}, u32[]{:S(2)}) copy-start(bf16[1,32,2304]{2,1,0:T(8,128)(2,1)} %param.12) | copy-start | bytes 442372
  1.5 0.9 %copy-start.2 = (bf16[1,32,2304]{2,1,0:T(8,128)(2,1)S(1)}, bf16[1,32,2304]{2,1,0:T(8,128)(2,1)}, u32[]{:S(2)}) copy-start(bf16[1,32,2304]{2,1,0:T(8,128)(2,1)} %param.13) | copy-start | bytes 442372
  2.5 0.9 %copy-start.3 = (bf16[1,32,2304]{2,1,0:T(8,128)(2,1)S(1)}, bf16[1,32,2304]{2,1,0:T(8,128)(2,1)}, u32[]{:S(2)}) copy-start(bf16[1,32,2304]{2,1,0:T(8,128)(2,1)} %param.11) | copy-start | bytes 442372
  3.4 0.7 %copy-start.4 = (f32[1,2304]{1,0:T(1,128)S(1)}, f32[1,2304]{1,0:T(1,128)}, u32[]{:S(2)}) copy-start(f32[1,2304]{1,0:T(1,128)} %stiff_hbm.1) | copy-start | bytes 27652
  4.1 0.7 %copy-start.5 = (f32[1,2304]{1,0:T(1,128)S(1)}, f32[1,2304]{1,0:T(1,128)}, u32[]{:S(2)}) copy-start(f32[1,2304]{1,0:T(1,128)} %record_hbm.1) | copy-start | bytes 27652
  4.8 0.7 %copy-start.6 = (s32[1,18,128]{2,0,1:T(1,128)S(1)}, s32[1,18,128]{2,0,1:T(1,128)}, u32[]{:S(2)}) copy-start(s32[1,18,128]{2,0,1:T(1,128)} %param.17) | copy-start | bytes 27652
  5.5 0.7 %copy-start.7 = (s32[1,18,18]{2,0,1:T(1,128)S(1)}, s32[1,18,18]{2,0,1:T(1,128)}, u32[]{:S(2)}) copy-start(s32[1,18,18]{2,0,1:T(1,128)} %param.10) | copy-start | bytes 3892
  6.2 0.7 copy-start.8
  7.6 7.9 %collective-permute-start = (bf16[9,32,128]{2,1,0:T(8,128)(2,1)S(1)}, bf16[9,32,128]{2,1,0:T(8,128)(2,1)S(1)}, u32[]{:S(2)}, u32[]{:S(2)}) collective-permute-start(bf16[9,32,128]{2,1,0:T(8,128)(2,1)S(1)} %get-tuple-element.29.own0_ref), channel_id=1, source_target_pairs={{0,1},{1,0},{2,3},{3,2},{4,5},{5,4},{6,7},{7,6},{8,9},{9,8},{10,11... | collective-permute-start | bytes 221192 | tf_op jit(solution)/shard_map/ppermute | solution.py:243
  8.9 6.6 %collective-permute-start.1 = (bf16[9,32,128]{2,1,0:T(8,128)(2,1)S(1)}, bf16[9,32,128]{2,1,0:T(8,128)(2,1)S(1)}, u32[]{:S(2)}, u32[]{:S(2)}) collective-permute-start(bf16[9,32,128]{2,1,0:T(8,128)(2,1)S(1)} %get-tuple-element.30.own1_ref), channel_id=1, source_target_pairs={{0,1},{1,0},{2,3},{3,2},{4,5},{5,4},{6,7},{7,6},{8,9},{9,8},{10,11... | collective-permute-start | bytes 221192 | tf_op jit(solution)/shard_map/ppermute | solution.py:243
  9.1 4.0 %copy-start = (bf16[1,18,18,128,128]{4,3,2,1,0:T(8,128)(2,1)S(1)}, bf16[1,18,18,128,128]{4,3,2,1,0:T(8,128)(2,1)}, u32[]{:S(2)}) copy-start(bf16[1,18,18,128,128]{4,3,2,1,0:T(8,128)(2,1)} %param.9) | copy-start | bytes 31850500
  20.4 4.4 %collective-permute-start.2 = (f32[9,40,128]{2,1,0:T(8,128)S(1)}, f32[9,40,128]{2,1,0:T(8,128)S(1)}, u32[]{:S(2)}, u32[]{:S(2)}) collective-permute-start(f32[9,40,128]{2,1,0:T(8,128)S(1)} %shard_map.107.own_ref), channel_id=1, source_target_pairs={{0,2},{2,0},{4,6},{6,4},{8,10},{10,8},{12,14},{14,12},{16,18},{18,... | collective-permute-start | bytes 552968 | tf_op jit(solution)/shard_map/ppermute | solution.py:254
  21.7 8.8 %collective-permute-start.3 = (f32[9,40,128]{2,1,0:T(8,128)S(1)}, f32[9,40,128]{2,1,0:T(8,128)S(1)}, u32[]{:S(2)}, u32[]{:S(2)}) collective-permute-start(f32[9,40,128]{2,1,0:T(8,128)S(1)} %shard_map.106.refs_0_.own_ref), channel_id=1, source_target_pairs={{0,0},{2,4},{4,2},{6,8},{8,6},{10,12},{12,10},{14,16},{16,14},{18,... | collective-permute-start | bytes 552968 | tf_op jit(solution)/shard_map/ppermute | solution.py:254
  25.6 7.0 %collective-permute-start.4 = (bf16[9,32,128]{2,1,0:T(8,128)(2,1)S(1)}, bf16[9,32,128]{2,1,0:T(8,128)(2,1)S(1)}, u32[]{:S(2)}, u32[]{:S(2)}) collective-permute-start(bf16[9,32,128]{2,1,0:T(8,128)(2,1)S(1)} %get-tuple-element.36.own0_ref), channel_id=1, source_target_pairs={{0,1},{1,0},{2,3},{3,2},{4,5},{5,4},{6,7},{7,6},{8,9},{9,8},{10,11... | collective-permute-start | bytes 221192 | tf_op jit(solution)/shard_map/ppermute | solution.py:243
  31.4 3.6 %collective-permute-start.5 = (bf16[9,32,128]{2,1,0:T(8,128)(2,1)S(1)}, bf16[9,32,128]{2,1,0:T(8,128)(2,1)S(1)}, u32[]{:S(2)}, u32[]{:S(2)}) collective-permute-start(bf16[9,32,128]{2,1,0:T(8,128)(2,1)S(1)} %get-tuple-element.37.own1_ref), channel_id=1, source_target_pairs={{0,1},{1,0},{2,3},{3,2},{4,5},{5,4},{6,7},{7,6},{8,9},{9,8},{10,11... | collective-permute-start | bytes 221192 | tf_op jit(solution)/shard_map/ppermute | solution.py:243
  39.8 2.7 %collective-permute-start.6 = (f32[9,32,128]{2,1,0:T(8,128)S(1)}, f32[9,32,128]{2,1,0:T(8,128)S(1)}, u32[]{:S(2)}, u32[]{:S(2)}) collective-permute-start(f32[9,32,128]{2,1,0:T(8,128)S(1)} %shard_map.111.own_ref), channel_id=1, source_target_pairs={{0,2},{2,0},{4,6},{6,4},{8,10},{10,8},{12,14},{14,12},{16,18},{18,... | collective-permute-start | bytes 442376 | tf_op jit(solution)/shard_map/ppermute | solution.py:254
  40.2 8.3 %collective-permute-start.7 = (f32[9,32,128]{2,1,0:T(8,128)S(1)}, f32[9,32,128]{2,1,0:T(8,128)S(1)}, u32[]{:S(2)}, u32[]{:S(2)}) collective-permute-start(f32[9,32,128]{2,1,0:T(8,128)S(1)} %shard_map.110.refs_0_.own_ref), channel_id=1, source_target_pairs={{0,0},{2,4},{4,2},{6,8},{8,6},{10,12},{12,10},{14,16},{16,14},{18,... | collective-permute-start | bytes 442376 | tf_op jit(solution)/shard_map/ppermute | solution.py:254
  43.3 7.3 %collective-permute-start.8 = (bf16[9,32,128]{2,1,0:T(8,128)(2,1)S(1)}, bf16[9,32,128]{2,1,0:T(8,128)(2,1)S(1)}, u32[]{:S(2)}, u32[]{:S(2)}) collective-permute-start(bf16[9,32,128]{2,1,0:T(8,128)(2,1)S(1)} %get-tuple-element.42.own0_ref), channel_id=1, source_target_pairs={{0,1},{1,0},{2,3},{3,2},{4,5},{5,4},{6,7},{7,6},{8,9},{9,8},{10,11... | collective-permute-start | bytes 221192 | tf_op jit(solution)/shard_map/ppermute | solution.py:243
  49.3 4.0 %collective-permute-start.9 = (bf16[9,32,128]{2,1,0:T(8,128)(2,1)S(1)}, bf16[9,32,128]{2,1,0:T(8,128)(2,1)S(1)}, u32[]{:S(2)}, u32[]{:S(2)}) collective-permute-start(bf16[9,32,128]{2,1,0:T(8,128)(2,1)S(1)} %get-tuple-element.45.own1_ref), channel_id=1, source_target_pairs={{0,1},{1,0},{2,3},{3,2},{4,5},{5,4},{6,7},{7,6},{8,9},{9,8},{10,11... | collective-permute-start | bytes 221192 | tf_op jit(solution)/shard_map/ppermute | solution.py:243
  58.2 2.4 %collective-permute-start.10 = (f32[9,32,128]{2,1,0:T(8,128)S(1)}, f32[9,32,128]{2,1,0:T(8,128)S(1)}, u32[]{:S(2)}, u32[]{:S(2)}) collective-permute-start(f32[9,32,128]{2,1,0:T(8,128)S(1)} %shard_map.115.own0_ref), channel_id=1, source_target_pairs={{0,2},{2,0},{4,6},{6,4},{8,10},{10,8},{12,14},{14,12},{16,18},{18,... | collective-permute-start | bytes 442376 | tf_op jit(solution)/shard_map/ppermute | solution.py:254
  58.7 8.0 %collective-permute-start.11 = (f32[9,32,128]{2,1,0:T(8,128)S(1)}, f32[9,32,128]{2,1,0:T(8,128)S(1)}, u32[]{:S(2)}, u32[]{:S(2)}) collective-permute-start(f32[9,32,128]{2,1,0:T(8,128)S(1)} %shard_map.114.refs_0_.own1_ref), channel_id=1, source_target_pairs={{0,0},{2,4},{4,2},{6,8},{8,6},{10,12},{12,10},{14,16},{16,14},{18,... | collective-permute-start | bytes 442376 | tf_op jit(solution)/shard_map/ppermute | solution.py:254
